TPU v7x, 256 devices: a whole 4x4x8 slice. The times are simulated.
256 devices in a mesh: rep: 8 (over z_lo, core), shard: 32 (over z_hi, x, y).
Axes of the slice: x: 4, y: 4, z: 8 (z_hi: 2, z_lo: 4; z = z_hi * 4 + z_lo), core: 2. Of those that a mesh axis runs over, the one named last changes fastest.
Arguments:
- hidden: bfloat16 [16384, 3584], P(('rep', 'shard')), may hold values from -6 to 6
- norm_gain: float32 [3584], replicated, may hold values from 0.5 to 1.5
- input_ids: int32 [16384], replicated, may hold values from 0 to 16383
- sampled_ids: int32 [16384], replicated, may hold values from 0 to 16383
- head_weight: bfloat16 [3584, 16384], P(None, 'shard'), as said below
- moment: bfloat16 [3584, 16384], P('rep', 'shard'), may hold values from -0.29882812 to 0.29882812
- curvature: bfloat16 [3584, 16384], P('rep', 'shard'), may hold values from 0.049804688 to 5
Outputs:
- moment_new: bfloat16 [3584, 16384], P('rep', 'shard')
- curvature_new: bfloat16 [3584, 16384], P('rep', 'shard')
- update_direction: bfloat16 [3584, 16384], P('rep', 'shard')
Inputs may be any that keep to these rules, and one draw needn't show every extreme that they name: Entries of head_weight are finite.
All inputs are finite; a program needn't handle non-finite values.
Results may differ from a plain program's by a relative error of at most 0.039.
Values may be sent and summed in bfloat16 or wider, within the bound.
A program may use at most 192 MiB of HBM per device.

v0:
```python
import jax
import jax.numpy as jnp
from jax import lax
from jax.sharding import PartitionSpec as P

EPS_NORM = 1e-05
BETA_ONE = 0.96
BETA_TWO = 0.95
RHO_SCALE = 0.05


def normalize(hidden, norm_gain):
    values = hidden.astype(jnp.float32)
    row_scale = lax.rsqrt(jnp.mean(values * values, axis=-1, keepdims=True) + EPS_NORM)
    return (values * row_scale * norm_gain).astype(jnp.bfloat16)


def local_targets(token_ids, sample_ids, first_col, columns):
    row_count = token_ids.shape[0]
    position = jnp.arange(row_count)
    shifted = jnp.roll(token_ids, -1) - first_col
    usable = (position < row_count - 1) & (shifted >= 0) & (shifted < columns)
    true_slot = jnp.where(usable, shifted, columns)
    sample_local = sample_ids - first_col
    inside = (sample_local >= 0) & (sample_local < columns)
    sample_slot = jnp.where(inside, sample_local, columns)
    return (true_slot, sample_slot)


def group_partial(feature_rows, probabilities, true_slot, sample_slot, columns):
    shared = lax.dot_general(
        feature_rows, probabilities, (((0,), (0,)), ((), ())), preferred_element_type=jnp.float32
    )
    widened = feature_rows.astype(jnp.float32)
    true_sums = jax.ops.segment_sum(widened, true_slot, num_segments=columns + 1)[:columns]
    sample_sums = jax.ops.segment_sum(widened, sample_slot, num_segments=columns + 1)[:columns]
    true_part = (shared - true_sums.T).astype(jnp.bfloat16)
    sample_part = (shared - sample_sums.T).astype(jnp.bfloat16)
    return (true_part, sample_part)


def on_device(hidden, norm_gain, input_ids, sampled_ids, head_weight, moment, curvature):
    normed = normalize(hidden, norm_gain)
    gathered = lax.all_gather(normed, "shard", axis=0, tiled=True)
    group_len = gathered.shape[0]
    columns = head_weight.shape[1]
    first_col = lax.axis_index("shard") * columns
    logits = jnp.dot(gathered, head_weight, preferred_element_type=jnp.float32)
    local_peak = jnp.max(logits, axis=-1)
    row_peak = lax.pmax(local_peak, "shard")
    scaled_exp = jnp.exp(logits - row_peak[:, None])
    row_sum = lax.psum(jnp.sum(scaled_exp, axis=-1), "shard")
    probabilities = scaled_exp / row_sum[:, None]
    probabilities = probabilities.astype(jnp.bfloat16)
    group_start = lax.axis_index("rep") * group_len
    token_ids = lax.dynamic_slice_in_dim(input_ids, group_start, group_len, 0)
    sample_ids = lax.dynamic_slice_in_dim(sampled_ids, group_start, group_len, 0)
    true_slot, sample_slot = local_targets(token_ids, sample_ids, first_col, columns)
    true_part, sample_part = group_partial(gathered, probabilities, true_slot, sample_slot, columns)
    gradient, sample_grad = (
        lax.psum_scatter(true_part, "rep", scatter_dimension=0, tiled=True).astype(jnp.float32),
        lax.psum_scatter(sample_part, "rep", scatter_dimension=0, tiled=True).astype(jnp.float32),
    )
    moment_new = BETA_ONE * moment.astype(jnp.float32) + (1.0 - BETA_ONE) * gradient
    curvature_new = (
        BETA_TWO * curvature.astype(jnp.float32) + (1.0 - BETA_TWO) * sample_grad * sample_grad
    )
    update_direction = jnp.clip(moment_new / (RHO_SCALE * curvature_new), -1.0, 1.0)
    return (
        moment_new.astype(jnp.bfloat16),
        curvature_new.astype(jnp.bfloat16),
        update_direction.astype(jnp.bfloat16),
    )


def solution(mesh):
    in_specs = (
        P(("rep", "shard"), None),
        P(),
        P(),
        P(),
        P(None, "shard"),
        P("rep", "shard"),
        P("rep", "shard"),
    )
    out_specs = (P("rep", "shard"), P("rep", "shard"), P("rep", "shard"))
    return jax.shard_map(
        on_device, mesh=mesh, in_specs=in_specs, out_specs=out_specs, check_vma=False
    )
```

profile of v0, /device:TPU:1, one launch (start us, length us, event | category | flops | bytes accessed | tf_op | source)
XLA Modules:
  0.0 722.6 jit_solution(855497205578411881)
XLA Ops:
  7.2 1.2 fusion.12
  8.4 2.0 fusion.14
  10.4 0.0 reduce-scatter.3.cloned.1.call-start
  10.5 1.3 dynamic-slice.1
  11.8 0.8 dynamic-slice
  12.5 0.7 and_select_fusion.1
  13.2 0.7 and_select_fusion
  14.0 224.5 %all-gather.2.cloned.1.call-done = bf16[2048,3584]{1,0:T(8,128)(2,1)} async-done(((bf16[64,3584]{1,0:T(8,128)(2,1)}), bf16[2048,3584]{1,0:T(8,128)(2,1)}) %all-gather.2.cloned.1.call-update) | async-done | bytes 14680080 | tf_op jit(solution)/shard_map/all_gather | solution.py:44
  238.5 45.2 %scatter_custom_fusion = f32[513,3584]{1,0:T(8,128)} fusion(s32[2048]{0:T(1024)S(1)} %bitcast.15, bf16[2048,3584]{1,0:T(8,128)(2,1)} %all-gather.2.cloned.1.call-done, f32[]{:T(128)} %constant.19.clone.1), kind=kCustom, calls=%fused_computation.4 | custom fusion | flops 14680064 | bytes 22034436 | tf_op jit(solution)/shard_map/scatter-add | solution.py:35
  283.7 6.5 slice.18
  290.2 8.4 %copy.13 = f32[512,3584]{0,1:T(8,128)} copy(f32[512,3584]{1,0:T(8,128)} %slice.18) | data formatting | bytes 14680064
  298.6 45.2 %scatter_custom_fusion.1 = f32[513,3584]{1,0:T(8,128)} fusion(s32[2048]{0:T(1024)S(1)} %and_select_fusion.1, bf16[2048,3584]{1,0:T(8,128)(2,1)} %all-gather.2.cloned.1.call-done, f32[]{:T(128)} %constant.19.clone.1), kind=kCustom, calls=%fused_computation.2 | custom fusion | flops 14680064 | bytes 22034436 | tf_op jit(solution)/shard_map/scatter-add | solution.py:36
  343.8 6.5 slice.19
  350.4 8.4 %copy.14 = f32[512,3584]{0,1:T(8,128)} copy(f32[512,3584]{1,0:T(8,128)} %slice.19) | data formatting | bytes 14680064
  358.7 13.5 %fusion.18 = (f32[2048]{0:T(1024)S(1)}, f32[2048,512]{0,1:T(8,128)}) fusion(bf16[2048,3584]{1,0:T(8,128)(2,1)} %all-gather.2.cloned.1.call-done, bf16[3584,512]{1,0:T(8,128)(2,1)} %param.11), kind=kOutput, calls=%fused_computation.34 | convolution fusion | flops 7517239296 | bytes 22552576 | tf_op jit(solution)/shard_map/dot_general | solution.py:48
  372.2 96.3 %pmax.7 = f32[2048]{0:T(1024)S(1)} all-reduce(f32[2048]{0:T(1024)S(1)} %get-tuple-element.8), channel_id=1, replica_groups=mesh['rep'=8,'shard'=32] {'shard'}, use_global_device_ids=true, to_apply=%region_2.0 | all-reduce | flops 2048 | bytes 16384 | tf_op jit(solution)/shard_map/pmax | solution.py:50
  468.5 2.8 fusion.8
  471.2 96.1 %psum.7 = f32[2048]{0:T(1024)S(1)} all-reduce(f32[2048]{0:T(1024)S(1)} %fusion.8), channel_id=1, replica_groups=mesh['rep'=8,'shard'=32] {'shard'}, use_global_device_ids=true, to_apply=%region_4.0 | all-reduce | flops 2048 | bytes 16384 | tf_op jit(solution)/shard_map/psum | solution.py:52
  567.4 19.4 %fusion.4 = (bf16[3584,512]{1,0:T(8,128)(2,1)}, bf16[3584,512]{1,0:T(8,128)(2,1)}) fusion(f32[512,3584]{0,1:T(8,128)} %copy.14, f32[512,3584]{0,1:T(8,128)} %copy.13, bf16[2048,3584]{1,0:T(8,128)(2,1)} %all-gather.2.cloned.1.call-done, f32[2048,512]{0,1:T(8,128)} %get-tuple-element.9, f32[2048]{0:T(1024)S(1)} %psum.7, f32[2048]{0:T(1024)S(1)} %pmax.7), kind=kOutput, calls=%fused_computation.7 | convolution fusion | flops 7526678528 | bytes 40910848 | tf_op jit(solution)/shard_map/dot_general | solution.py:31
  586.8 0.0 reduce-scatter.5.cloned.1.call-start
  586.8 0.7 reduce-scatter.5.cloned.1.call-update
  587.5 74.1 %reduce-scatter.3.cloned.1.call-done = bf16[448,512]{1,0:T(8,128)(2,1)} async-done(((bf16[3584,512]{1,0:T(8,128)(2,1)}), bf16[448,512]{1,0:T(8,128)(2,1)}) %reduce-scatter.3.cloned.1.call-update) | async-done | bytes 458768 | tf_op jit(solution)/shard_map/reduce_scatter | solution.py:61
  661.7 51.8 %reduce-scatter.5.cloned.1.call-done = bf16[448,512]{1,0:T(8,128)(2,1)} async-done(((bf16[3584,512]{1,0:T(8,128)(2,1)}), bf16[448,512]{1,0:T(8,128)(2,1)}) %reduce-scatter.5.cloned.1.call-update) | async-done | bytes 458768 | tf_op jit(solution)/shard_map/reduce_scatter | solution.py:62
  713.5 2.6 clamp_convert_fusion
  (8 shorter events, 0.1 us)
Async XLA Ops:
  7.2 231.3 %all-gather.2.cloned.1.call-start = ((), (), s32[]{:S(2)}) async-start(), calls=%async_computation.2 | async-start | bytes 15138816 | tf_op jit(solution)/shard_map/all_gather | solution.py:44
  10.4 651.2 %reduce-scatter.3.cloned.1.call-start = ((), (), s32[]{:S(2)}) async-start(), calls=%async_computation.3 | async-start | bytes 4128768 | tf_op jit(solution)/shard_map/reduce_scatter | solution.py:61
  586.8 126.7 %copy-start = (bf16[448,512]{1,0:T(8,128)(2,1)S(1)}, bf16[448,512]{1,0:T(8,128)(2,1)}, u32[]{:S(2)}) copy-start(bf16[448,512]{1,0:T(8,128)(2,1)} %param.12) | copy-start | bytes 1376260
  586.8 126.7 %copy-start.1 = (bf16[448,512]{1,0:T(8,128)(2,1)S(1)}, bf16[448,512]{1,0:T(8,128)(2,1)}, u32[]{:S(2)}) copy-start(bf16[448,512]{1,0:T(8,128)(2,1)} %param.13) | copy-start | bytes 1376260
  586.8 126.7 %reduce-scatter.5.cloned.1.call-start = ((), (), s32[]{:S(2)}) async-start(), calls=%async_computation.4 | async-start | bytes 4128768 | tf_op jit(solution)/shard_map/reduce_scatter | solution.py:62
Sparse Core Ops, SparseCore 0:
  12.0 226.4 all-gather.1
  586.9 74.7 reduce-scatter.2
  664.2 49.1 reduce-scatter.4
where the time goes:
time: 725 us; the launch traced here: 723 us
  waiting for transfers between devices  351 us (48%)
  blocking collectives  192 us (26%)
  other arithmetic  100 us (14%)
  matrix products  32.9 us (5%)
  local copies, waits for them, and re-layouts  31.8 us (4%)
  between operations  13.8 us (2%)
    all_gather x1, waiting for transfers between devices, on_device(): gathered = lax.all_gather(normed, 'shard', axis=0, tiled=True)  225 us
    pmax x1, blocking collectives, on_device(): row_peak = lax.pmax(local_peak, 'shard')  96.3 us
    psum x1, blocking collectives, on_device(): row_sum = lax.psum(jnp.sum(scaled_exp, axis=-1), 'shard')  96.1 us
    reduce_scatter x1, waiting for transfers between devices, on_device(): lax.psum_scatter(true_part, 'rep', scatter_dimension=0, tiled=True)  74.1 us
    reduce_scatter x1, waiting for transfers between devices, on_device(): lax.psum_scatter(sample_part, 'rep', scatter_dimension=0, tiled=True)  51.8 us
    scatter-add x1, other arithmetic, group_partial(): jax.ops.segment_sum(widened, true_slot, num_segments=columns + 1)[:columns]  45.2 us
    scatter-add x1, other arithmetic, group_partial(): jax.ops.segment_sum(widened, sample_slot, num_segments=columns + 1)  45.2 us
    dot_general x1, matrix products, group_partial(): lax.dot_general(feature_rows, probabilities, (((0,), (0,)), ((), ())), pr...  19.4 us
  transfers between devices with their start and end apart: 3, of which 3 were waited for; matrix products, arithmetic and copies ran while one was open for 0% of the time, Pallas kernels for 0%

commit v1 on v0

v1 whole, which is shorter than its diff:
```python
import jax
import jax.numpy as jnp
from jax import lax
from jax.experimental import pallas as pl
from jax.experimental.pallas import tpu as pltpu
from jax.sharding import PartitionSpec as P

EPS_NORM = 1e-05
BETA_ONE = 0.96
BETA_TWO = 0.95
RHO_SCALE = 0.05

NX = NY = 4
Z_LO, Z_HI, CORES = 4, 2, 2
NZ = Z_HI * Z_LO
PLANE = NX * NY
TILES = 2 * 4
BF16, F32 = jnp.bfloat16, jnp.float32
MESH = pl.DeviceIdType.MESH


class Sizes:
    def __init__(self, rows, features, columns, state_rows):
        self.rows = rows
        self.half = rows // 2
        self.part = rows // 4
        self.features = features
        self.columns = columns
        self.tile = 4 * CORES * self.half
        self.tokens = TILES * self.tile
        self.state_rows = state_rows
        self.quarter = CORES * state_rows
        self.weight_chunks = 8


def kernel(
    sz, hidden, gain, tgt, smp, weight, moment, curvature, moment_out, curvature_out, update_out,
    normed, w_buf, w_t, expd, probs, ring, part_sum, totals, mine_out,
    st_own, st_one, st_mid, st_two, factor,
    ag_send, ag_recv, sib_send, sib_recv, w_send, w_recv, w_local, s1_send, s1_recv, s2_send, s2_recv,
    rs_send, rs_recv, fin_send, fin_recv,
):
    rep, shard = lax.axis_index("rep"), lax.axis_index("shard")
    z_lo, core = rep // CORES, rep % CORES
    z_hi, x, y = shard // PLANE, (shard // NY) % NX, shard % NY
    z = z_hi * Z_LO + z_lo
    native = core == z_hi

    def device(dx=0, dy=0, dz=0, dc=0):
        xx, yy, zz, cc = (x + dx) % NX, (y + dy) % NY, (z + dz) % NZ, (core + dc) % CORES
        return ((zz % Z_LO) * CORES + cc, (zz // Z_LO) * PLANE + xx * NY + yy)

    row_peers = [(dx, dc) for dx in range(NX) for dc in range(CORES) if (dx, dc) != (0, 0)]
    column_peers = [1, 2, 3]
    barrier = pltpu.get_barrier_semaphore()
    partners = [device(dx=dx, dc=dc) for dx, dc in row_peers]
    partners += [device(dy=dy) for dy in column_peers]
    partners += [device(dz=1), device(dz=NZ - 1)]
    for partner in partners:
        pl.semaphore_signal(barrier, inc=1, device_id=partner, device_id_type=MESH)

    def block_row(h, da, db, cc):
        a, b = (x, y) if h == 0 else (y, x)
        return ((h * 4 + (b + db) % 4) * 4 + (a + da) % 4) * (CORES * sz.half) + cc * sz.half

    w_copy = pltpu.make_async_copy(weight, w_buf, w_local)

    @pl.when(native)
    def _():
        w_copy.start()

    for h in range(2):
        values = hidden[pl.ds(h * sz.half, sz.half), :].astype(F32)
        scale = lax.rsqrt(jnp.mean(values * values, axis=-1, keepdims=True) + EPS_NORM)
        rows = pl.ds(pl.multiple_of(block_row(h, 0, 0, core), sz.half), sz.half)
        normed[rows, :] = (values * scale * gain[...]).astype(BF16)
    pl.semaphore_wait(barrier, len(partners))

    sent = []

    def start(copy):
        copy.start()
        sent.append(copy)

    def ag_copy(h, da, db, part, along, step, index):
        to_a, to_b = (step, 0) if along == 0 else (0, step)
        dx, dy = (to_a, to_b) if h == 0 else (to_b, to_a)
        first = block_row(h, da, db, core)
        if part is None:
            rows = pl.ds(pl.multiple_of(first, sz.half), sz.half)
        else:
            rows = pl.ds(pl.multiple_of(first + part * sz.part, sz.part), sz.part)
        block = normed.at[rows]
        return pltpu.make_async_remote_copy(
            src_ref=block, dst_ref=block, send_sem=ag_send.at[h, index],
            recv_sem=ag_recv.at[h, (da - to_a) % 4, (db - to_b) % 4, part or 0],
            device_id=device(dx=dx, dy=dy), device_id_type=MESH,
        )

    counts = [0, 0]

    def ag_send_block(h, da, db, part, along, step):
        start(ag_copy(h, da % 4, db % 4, part, along, step, counts[h]))
        counts[h] += 1

    def ag_wait(h, da, db):
        da, db = da % 4, db % 4
        first = block_row(h, da, db, core)
        split = da == 2 if db == 0 else db == 2
        for part in (0, 1) if split else (None,):
            if part is None:
                rows = pl.ds(pl.multiple_of(first, sz.half), sz.half)
            else:
                rows = pl.ds(pl.multiple_of(first + part * sz.part, sz.part), sz.part)
            pltpu.make_async_remote_copy(
                src_ref=normed.at[rows], dst_ref=normed.at[rows], send_sem=ag_send.at[h, 0],
                recv_sem=ag_recv.at[h, da, db, part or 0], device_id=device(dx=1), device_id_type=MESH,
            ).wait_recv()

    def sib_copy(h, da, db, cc):
        rows = pl.ds(pl.multiple_of(block_row(h, da, db, cc), sz.half), sz.half)
        return pltpu.make_async_remote_copy(
            src_ref=normed.at[rows], dst_ref=normed.at[rows], send_sem=sib_send.at[h, (da % 4) * 4 + db % 4],
            recv_sem=sib_recv.at[h, (da % 4) * 4 + db % 4], device_id=device(dc=1), device_id_type=MESH,
        )

    def to_sibling(h, da, db):
        start(sib_copy(h, da, db, core))

    chunk = sz.features // sz.weight_chunks
    up_chunks = sz.weight_chunks // 2

    def w_copy_of(way, j, source):
        rows = pl.ds((way * up_chunks + j) * chunk, chunk)
        return pltpu.make_async_remote_copy(
            src_ref=source.at[rows], dst_ref=w_buf.at[rows], send_sem=w_send.at[way, j], recv_sem=w_recv.at[way, j],
            device_id=device(dz=1 if way == 0 else NZ - 1), device_id_type=MESH,
        )

    ends = [Z_LO - 1, 0]

    def w_first():
        for way in range(2):

            @pl.when(native & (z_lo == ends[way]))
            def _():
                for j in range(up_chunks):
                    w_copy_of(way, j, weight).start()

    def w_step(j):
        @pl.when(jnp.logical_not(native))
        def _():
            for way in range(2):
                w_copy_of(way, j, w_buf).wait_recv()

                @pl.when(z_lo != ends[way])
                def _():
                    w_copy_of(way, j, w_buf).start()

    def w_finish():
        for way in range(2):

            @pl.when((native & (z_lo == ends[way])) | (jnp.logical_not(native) & (z_lo != ends[way])))
            def _():
                for j in range(up_chunks):
                    w_copy_of(way, j, w_buf).wait_send()

    def logits_tile(t):
        rows = pl.ds(pl.multiple_of(t * sz.tile, sz.tile), sz.tile)
        logits = lax.dot_general(
            w_t[...], normed[rows, :], (((1,), (1,)), ((), ())), preferred_element_type=F32
        )
        peak = jnp.max(logits, axis=0, keepdims=True)
        scaled = jnp.exp(logits - peak)
        expd[t] = scaled
        st_own[pl.ds(t, 1), :] = peak
        st_own[pl.ds(TILES + t, 1), :] = jnp.sum(scaled, axis=0, keepdims=True)

    def two_tiles(offset):
        for h in range(2):
            for da in range(4):
                sib_copy(h, da, offset, core).wait_recv()

        def body(h, carry):
            logits_tile(h * 4 + jnp.where(h == 0, y + offset, x + offset) % 4)
            return carry

        lax.fori_loop(0, 2, body, 0)

    w_first()
    for h in range(2):
        for step in (1, -1):
            ag_send_block(h, 0, 0, None, 0, step)
    for h in range(2):
        for step in (1, -1):
            ag_send_block(h, 0, 0, None, 1, step)
        to_sibling(h, 0, 0)

    def forward_a(h):
        for da in (-1, 1):
            ag_wait(h, da, 0)
            ag_send_block(h, da, 0, 0 if da == -1 else 1, 0, -da)
        for da in (-1, 1):
            for step in (1, -1):
                ag_send_block(h, da, 0, None, 1, step)
            to_sibling(h, da, 0)

    def across_a(h):
        ag_wait(h, 2, 0)
        for step in (1, -1):
            ag_send_block(h, 2, 0, None, 1, step)
        to_sibling(h, 2, 0)

    def forward_b(h, da):
        for db in (-1, 1):
            ag_wait(h, da, db)
            ag_send_block(h, da, db, 0 if db == -1 else 1, 1, -db)
            to_sibling(h, da, db)

    def across_b(h, da):
        ag_wait(h, da, 2)
        to_sibling(h, da, 2)

    for h in range(2):
        forward_a(h)
    w_step(0)
    for h in range(2):
        forward_b(h, 0)
    for h in range(2):
        across_a(h)
    w_step(1)
    for h in range(2):
        forward_b(h, -1)
    w_step(2)
    for h in range(2):
        forward_b(h, 1)
    w_step(3)
    for h in range(2):
        across_b(h, 0)

    @pl.when(native)
    def _():
        w_copy.wait()

    slab = sz.columns

    def turn(j, carry):
        first = pl.multiple_of(j * slab, slab)
        w_t[:, pl.ds(first, slab)] = w_buf[pl.ds(first, slab), :].T
        return carry

    lax.fori_loop(0, sz.features // slab, turn, 0)
    two_tiles(0)
    for h in range(2):
        forward_b(h, 2)
    two_tiles(1)
    two_tiles(-1)
    for h in range(2):
        across_b(h, -1)
        across_b(h, 1)
    for h in range(2):
        across_b(h, 2)
    two_tiles(2)

    def join(pairs):
        peak = pairs[0][0]
        for other, _ in pairs[1:]:
            peak = jnp.maximum(peak, other)
        total = 0.0
        for other, part in pairs:
            total = total + part * jnp.exp(other - peak)
        return peak, total

    def pair(ref):
        return ref[:TILES, :], ref[TILES:, :]

    ones = [
        pltpu.make_async_remote_copy(
            src_ref=st_own, dst_ref=st_one.at[j], send_sem=s1_send.at[j], recv_sem=s1_recv.at[j],
            device_id=device(dx=dx, dc=dc), device_id_type=MESH,
        )
        for j, (dx, dc) in enumerate(row_peers)
    ]
    for copy in ones:
        start(copy)
    for copy in ones:
        copy.wait_recv()
    peak, total = join([pair(st_own)] + [pair(st_one.at[j]) for j in range(len(row_peers))])
    st_mid[:TILES, :] = peak
    st_mid[TILES:, :] = total
    twos = [
        pltpu.make_async_remote_copy(
            src_ref=st_mid, dst_ref=st_two.at[j], send_sem=s2_send.at[j], recv_sem=s2_recv.at[j],
            device_id=device(dy=dy), device_id_type=MESH,
        )
        for j, dy in enumerate(column_peers)
    ]
    for copy in twos:
        start(copy)
    for copy in twos:
        copy.wait_recv()
    peak, total = join([pair(st_mid)] + [pair(st_two.at[j]) for j in range(len(column_peers))])
    factor[...] = jnp.exp(st_own[:TILES, :] - peak) / total

    def probs_tile(t, carry):
        scaled = expd[t] * factor[pl.ds(t, 1), :]
        column = lax.broadcasted_iota(jnp.int32, (sz.columns, sz.tile), 0)
        lanes = pl.ds(pl.multiple_of(t * sz.tile, sz.tile), sz.tile)
        for d, labels in enumerate((tgt, smp)):
            hit = column == labels[pl.ds(t, 1), :]
            probs[d, :, lanes] = jnp.where(hit, scaled - 1.0, scaled).astype(BF16)
        return carry

    lax.fori_loop(0, TILES, probs_tile, 0)

    sub = sz.columns // 2

    def rs_copy(d, slot, u):
        block = ring.at[d, slot, u]
        return pltpu.make_async_remote_copy(
            src_ref=block, dst_ref=block, send_sem=rs_send.at[d, slot, u], recv_sem=rs_recv.at[d, slot, u],
            device_id=device(dz=1 if d == 0 else NZ - 1), device_id_type=MESH,
        )

    def product(d, quarter):
        lanes = pl.ds(pl.multiple_of(quarter * sz.quarter, sz.quarter), sz.quarter)
        part_sum[d] = jnp.dot(probs[d], normed[:, lanes], preferred_element_type=F32)

    def owner(d, k):
        return (z + NZ - 1 - k) % NZ if d == 0 else (z + 1 + k) % NZ

    def hop(k, carry):
        for d in range(2):
            to = owner(d, k)

            @pl.when(to // Z_LO == core)
            def _():
                product(d, to % Z_LO)

        for d in range(2):
            to = owner(d, k)

            @pl.when(to // Z_LO == core)
            def _():
                slot = to % Z_LO
                for u in range(2):
                    rows = slice(u * sub, (u + 1) * sub)

                    @pl.when(k == 0)
                    def _():
                        ring[d, slot, u] = part_sum[d, rows, :].astype(BF16)

                    @pl.when(k > 0)
                    def _():
                        rs_copy(d, slot, u).wait_recv()
                        ring[d, slot, u] = (ring[d, slot, u].astype(F32) + part_sum[d, rows, :]).astype(BF16)

                    rs_copy(d, slot, u).start()

        return carry

    lax.fori_loop(0, NZ - 1, hop, 0)

    def fin_copy(cc):
        rows = pl.ds(pl.multiple_of(cc * sz.state_rows, sz.state_rows), sz.state_rows)
        return pltpu.make_async_remote_copy(
            src_ref=totals.at[:, rows], dst_ref=mine_out, send_sem=fin_send, recv_sem=fin_recv,
            device_id=device(dc=1), device_id_type=MESH,
        )

    @pl.when(native)
    def _():
        for d in range(2):
            product(d, z_lo)
        for d in range(2):
            for u in range(2):
                rows = slice(u * sub, (u + 1) * sub)
                rs_copy(d, z_lo, u).wait_recv()
                total = ring[d, z_lo, u].astype(F32) + part_sum[d, rows, :]
                totals[d, :, rows] = total.T.astype(BF16)
        fin_copy(1 - core).start()
        own = pl.ds(pl.multiple_of(core * sz.state_rows, sz.state_rows), sz.state_rows)
        mine_out[...] = totals[:, own, :]

    @pl.when(jnp.logical_not(native))
    def _():
        fin_copy(0).wait_recv()

    gradient, sample_grad = mine_out[0].astype(F32), mine_out[1].astype(F32)
    moment_new = BETA_ONE * moment[...].astype(F32) + (1.0 - BETA_ONE) * gradient
    curvature_new = BETA_TWO * curvature[...].astype(F32) + (1.0 - BETA_TWO) * sample_grad * sample_grad
    moment_out[...] = moment_new.astype(BF16)
    curvature_out[...] = curvature_new.astype(BF16)
    update_out[...] = jnp.clip(moment_new / (RHO_SCALE * curvature_new), -1.0, 1.0).astype(BF16)

    for copy in sent:
        copy.wait_send()
    w_finish()

    def drain(k, carry):
        for d in range(2):
            to = owner(d, k)

            @pl.when(to // Z_LO == core)
            def _():
                for u in range(2):
                    rs_copy(d, to % Z_LO, u).wait_send()

        return carry

    lax.fori_loop(0, NZ - 1, drain, 0)

    @pl.when(native)
    def _():
        fin_copy(0).wait_send()


def plane_labels(input_ids, sampled_ids, columns):
    rep, shard = lax.axis_index("rep"), lax.axis_index("shard")
    z_lo, core, z_hi, place = rep // CORES, rep % CORES, shard // PLANE, shard % PLANE
    tokens = input_ids.shape[0]
    span = tokens // (NZ * CORES)
    group = tokens // (Z_LO * CORES)
    first_col = (core * PLANE + place) * columns
    position = jnp.arange(tokens)
    targets = jnp.where(position % group < group - 1, jnp.roll(input_ids, -1), -1)

    def of_plane(ids):
        mine = ids.reshape(Z_LO, CORES, Z_HI, span)
        mine = lax.dynamic_slice(mine, (z_lo, 0, z_hi, 0), (1, CORES, 1, span))
        mine = mine.reshape(CORES, NX, NY, 2, -1)
        first = mine[:, :, :, 0].transpose(2, 1, 0, 3)
        second = mine[:, :, :, 1].transpose(1, 2, 0, 3)
        return jnp.concatenate([first, second]).reshape(TILES, -1)

    return of_plane(targets) - first_col, of_plane(sampled_ids) - first_col


def on_device(hidden, norm_gain, input_ids, sampled_ids, head_weight, moment, curvature):
    rows, features = hidden.shape
    columns = head_weight.shape[1]
    sz = Sizes(rows, features, columns, moment.shape[0])
    tgt, smp = plane_labels(input_ids, sampled_ids, columns)
    vmem = pl.BlockSpec(memory_space=pltpu.VMEM)
    state = jax.ShapeDtypeStruct(moment.shape, BF16)
    dma = pltpu.SemaphoreType.DMA
    n_chunks = sz.weight_chunks // 2
    return pl.pallas_call(
        lambda *refs: kernel(sz, *refs),
        out_shape=(state, state, state),
        in_specs=[vmem, vmem, vmem, vmem, pl.BlockSpec(memory_space=pl.ANY), vmem, vmem],
        out_specs=(vmem, vmem, vmem),
        scratch_shapes=[
            pltpu.VMEM((sz.tokens, features), BF16),
            pltpu.VMEM((features, columns), BF16),
            pltpu.VMEM((columns, features), BF16),
            pltpu.VMEM((TILES, columns, sz.tile), F32),
            pltpu.VMEM((2, columns, sz.tokens), BF16),
            pltpu.VMEM((2, Z_LO, 2, columns // 2, sz.quarter), BF16),
            pltpu.VMEM((2, columns, sz.quarter), F32),
            pltpu.VMEM((2, sz.quarter, columns), BF16),
            pltpu.VMEM((2, sz.state_rows, columns), BF16),
            pltpu.VMEM((2 * TILES, sz.tile), F32),
            pltpu.VMEM((7, 2 * TILES, sz.tile), F32),
            pltpu.VMEM((2 * TILES, sz.tile), F32),
            pltpu.VMEM((3, 2 * TILES, sz.tile), F32),
            pltpu.VMEM((TILES, sz.tile), F32),
            dma((2, 20)),
            dma((2, 4, 4, 2)),
            dma((2, 16)),
            dma((2, 16)),
            dma((2, n_chunks)),
            dma((2, n_chunks)),
            dma,
            dma((7,)),
            dma((7,)),
            dma((3,)),
            dma((3,)),
            dma((2, Z_LO, 2)),
            dma((2, Z_LO, 2)),
            dma,
            dma,
        ],
        compiler_params=pltpu.CompilerParams(
            collective_id=0, has_side_effects=True, vmem_limit_bytes=60 * 1024 * 1024
        ),
    )(hidden, norm_gain.reshape(1, -1), tgt, smp, head_weight, moment, curvature)


def solution(mesh):
    in_specs = (
        P(("rep", "shard"), None),
        P(),
        P(),
        P(),
        P(None, "shard"),
        P("rep", "shard"),
        P("rep", "shard"),
    )
    out_specs = (P("rep", "shard"), P("rep", "shard"), P("rep", "shard"))
    return jax.shard_map(
        on_device, mesh=mesh, in_specs=in_specs, out_specs=out_specs, check_vma=False
    )
```

time: 725 us -> 330 us (0.46)
  waiting for transfers between devices: 351 us -> 0 us
  Pallas kernels: 0 us -> 316 us
  blocking collectives: 192 us -> 0 us
  other arithmetic: 100 us -> 1.01 us
  matrix products: 32.9 us -> 0 us
  local copies, waits for them, and re-layouts: 31.8 us -> 11.5 us
  between operations: 13.8 us -> 0.8 us
    pallas_call x0 -> x1, Pallas kernels: none -> 316 us  [on_device(): pl.pallas_call(lambda *refs: kernel(sz, *refs), out_shape=(state, state,...]
    all_gather x1 -> x0, waiting for transfers between devices: 225 us -> none  [on_device(): gathered = lax.all_gather(normed, 'shard', axis=0, tiled=True)]
    reduce_scatter x2 -> x0, waiting for transfers between devices: 126 us -> none  [the longest x1 74.1 us: on_device(): lax.psum_scatter(true_part, 'rep', scatter_dimension=0, tiled=True)]
    pmax x1 -> x0, blocking collectives: 96.3 us -> none  [on_device(): row_peak = lax.pmax(local_peak, 'shard')]
    psum x1 -> x0, blocking collectives: 96.1 us -> none  [on_device(): row_sum = lax.psum(jnp.sum(scaled_exp, axis=-1), 'shard')]
    scatter-add x2 -> x0, other arithmetic: 90.5 us -> none  [the longest x1 45.2 us: group_partial(): jax.ops.segment_sum(widened, true_slot, num_segments=columns + 1)[:columns]]
    dot_general x2 -> x0, matrix products: 32.9 us -> none  [the longest x1 19.4 us: group_partial(): lax.dot_general(feature_rows, probabilities, (((0,), (0,)), ((), ())), pr...]
    slice x4, local copies, waits for them, and re-layouts: 15.1 us -> 2.18 us  [the longest x2 2.12 us: plane_labels(): jnp.roll(input_ids, -1)]
  transfers between devices with their start and end apart: 3 -> 0, of which waited for: 3 -> 0; matrix products, arithmetic and copies ran while one was open for 0% -> 0% of each run, Pallas kernels for 0% -> 0%
where the time goes in v1:
time: 330 us; the launch traced here: 329 us
  Pallas kernels  316 us (96%)
  local copies, waits for them, and re-layouts  11.5 us (3%)
    pallas_call x1, Pallas kernels, on_device(): pl.pallas_call(lambda *refs: kernel(sz, *refs), out_shape=(state, state,...  316 us

profile of v1, /device:TPU:1, one launch (start us, length us, event | category | flops | bytes accessed | tf_op | source)
XLA Modules:
  0.0 329.3 jit_solution(13847256757982934569)
XLA Ops:
  0.7 1.2 slice.21
  1.9 1.3 reshape.27.refs_1_
  3.3 0.9 reshape.29
  4.1 0.9 slice.20
  5.1 0.7 pad_add_fusion
  5.8 0.1 fusion.2
  5.9 0.1 dynamic-slice_reduce_fusion
  6.0 0.1 reshape.30
  6.2 0.7 sub.27.refs_3_
  6.9 0.1 reshape.28
  7.2 0.7 sub.25.refs_2_
  7.9 316.0 %shard_map.94 = (bf16[448,512]{1,0:T(8,128)(2,1)}, bf16[448,512]{1,0:T(8,128)(2,1)}, bf16[448,512]{1,0:T(8,128)(2,1)}) custom-call(bf16[64,3584]{1,0:T(8,128)(2,1)} %refs_0_.1, f32[1,3584]{1,0:T(1,128)} %reshape.27.refs_1_, s32[8,256]{1,0:T(8,128)} %sub.25.refs_2_, s32[8,256]{1,0:T(8,128)} %sub.27.refs_3_, bf16[3584,512]{1,0:T(8,128)(2,1)} %refs_4_.1, ...), custom_call_target="tpu_custom_call" | custom-call | tf_op jit(solution)/shard_map/pallas_call | solution.py:448
  323.9 1.8 copy.43
  325.7 1.8 copy.44
  327.5 1.8 copy.45
  (13 shorter events, 0.3 us)

commit v2 on v1

--- a/solution.py
+++ b/solution.py
@@ -14,6 +14,9 @@
 Z_LO, Z_HI, CORES = 4, 2, 2
 NZ = Z_HI * Z_LO
 PLANE = NX * NY
+W_SLACK = 3
+W_AHEAD = 4
+RING_PARTS = 4
 TILES = 2 * 4
 BF16, F32 = jnp.bfloat16, jnp.float32
 MESH = pl.DeviceIdType.MESH
@@ -26,16 +29,17 @@
         self.part = rows // 4
         self.features = features
         self.columns = columns
+        self.share = columns // CORES
         self.tile = 4 * CORES * self.half
         self.tokens = TILES * self.tile
         self.state_rows = state_rows
         self.quarter = CORES * state_rows
-        self.weight_chunks = 8
+        self.weight_chunks = 32
 
 
 def kernel(
-    sz, hidden, gain, tgt, smp, weight, moment, curvature, moment_out, curvature_out, update_out,
-    normed, w_buf, w_t, expd, probs, ring, part_sum, totals, mine_out,
+    sz, hidden, gain, tgt, smp, weight, mine_out,
+    normed, w_buf, w_t, expd, probs, ring, part_sum, totals, other,
     st_own, st_one, st_mid, st_two, factor,
     ag_send, ag_recv, sib_send, sib_recv, w_send, w_recv, w_local, s1_send, s1_recv, s2_send, s2_recv,
     rs_send, rs_recv, fin_send, fin_recv,
@@ -44,7 +48,6 @@
     z_lo, core = rep // CORES, rep % CORES
     z_hi, x, y = shard // PLANE, (shard // NY) % NX, shard % NY
     z = z_hi * Z_LO + z_lo
-    native = core == z_hi
 
     def device(dx=0, dy=0, dz=0, dc=0):
         xx, yy, zz, cc = (x + dx) % NX, (y + dy) % NY, (z + dz) % NZ, (core + dc) % CORES
@@ -63,11 +66,9 @@
         a, b = (x, y) if h == 0 else (y, x)
         return ((h * 4 + (b + db) % 4) * 4 + (a + da) % 4) * (CORES * sz.half) + cc * sz.half
 
-    w_copy = pltpu.make_async_copy(weight, w_buf, w_local)
-
-    @pl.when(native)
-    def _():
-        w_copy.start()
+    share = pl.ds(pl.multiple_of(core * sz.share, sz.share), sz.share)
+    w_copy = pltpu.make_async_copy(weight.at[:, share], w_buf.at[z_hi], w_local)
+    w_copy.start()
 
     for h in range(2):
         values = hidden[pl.ds(h * sz.half, sz.half), :].astype(F32)
@@ -130,10 +131,11 @@
     chunk = sz.features // sz.weight_chunks
     up_chunks = sz.weight_chunks // 2
 
-    def w_copy_of(way, j, source):
-        rows = pl.ds((way * up_chunks + j) * chunk, chunk)
+    def w_copy_of(way, j, half):
+        rows = pl.ds(pl.multiple_of((way * up_chunks + j) * chunk, chunk), chunk)
+        block = w_buf.at[half, rows]
         return pltpu.make_async_remote_copy(
-            src_ref=source.at[rows], dst_ref=w_buf.at[rows], send_sem=w_send.at[way, j], recv_sem=w_recv.at[way, j],
+            src_ref=block, dst_ref=block, send_sem=w_send.at[way, j], recv_sem=w_recv.at[way, j],
             device_id=device(dz=1 if way == 0 else NZ - 1), device_id_type=MESH,
         )
 
@@ -142,28 +144,40 @@
     def w_first():
         for way in range(2):
 
-            @pl.when(native & (z_lo == ends[way]))
+            @pl.when(z_lo == ends[way])
             def _():
-                for j in range(up_chunks):
-                    w_copy_of(way, j, weight).start()
-
-    def w_step(j):
-        @pl.when(jnp.logical_not(native))
-        def _():
-            for way in range(2):
-                w_copy_of(way, j, w_buf).wait_recv()
+                for j in range(W_AHEAD):
+                    w_copy_of(way, j, z_hi).start()
+
+    def w_step(beat):
+        for way in range(2):
+            j = beat - W_SLACK * (z_lo if way == 0 else Z_LO - 1 - z_lo)
+
+            @pl.when((j >= 0) & (j < up_chunks))
+            def _():
+                w_copy_of(way, j, 1 - z_hi).wait_recv()
 
                 @pl.when(z_lo != ends[way])
                 def _():
-                    w_copy_of(way, j, w_buf).start()
+                    w_copy_of(way, j, 1 - z_hi).start()
+
+            if beat + W_AHEAD < up_chunks:
+
+                @pl.when(z_lo == ends[way])
+                def _():
+                    w_copy_of(way, beat, z_hi).wait_send()
+                    w_copy_of(way, beat + W_AHEAD, z_hi).start()
 
     def w_finish():
         for way in range(2):
-
-            @pl.when((native & (z_lo == ends[way])) | (jnp.logical_not(native) & (z_lo != ends[way])))
-            def _():
-                for j in range(up_chunks):
-                    w_copy_of(way, j, w_buf).wait_send()
+            for j in range(up_chunks):
+                if j < up_chunks - W_AHEAD:
+
+                    @pl.when(z_lo != ends[way])
+                    def _():
+                        w_copy_of(way, j, z_hi).wait_send()
+                else:
+                    w_copy_of(way, j, z_hi).wait_send()
 
     def logits_tile(t):
         rows = pl.ds(pl.multiple_of(t * sz.tile, sz.tile), sz.tile)
@@ -187,10 +201,12 @@
 
         lax.fori_loop(0, 2, body, 0)
 
-    w_first()
     for h in range(2):
         for step in (1, -1):
             ag_send_block(h, 0, 0, None, 0, step)
+
+    w_copy.wait()
+    w_first()
     for h in range(2):
         for step in (1, -1):
             ag_send_block(h, 0, 0, None, 1, step)
@@ -221,43 +237,49 @@
         ag_wait(h, da, 2)
         to_sibling(h, da, 2)
 
+    beats = iter(range(up_chunks + W_SLACK * (Z_LO - 1)))
+
+    def w_beats(many):
+        for _ in range(many):
+            w_step(next(beats))
+
+    w_beats(3)
     for h in range(2):
         forward_a(h)
-    w_step(0)
+    w_beats(4)
     for h in range(2):
         forward_b(h, 0)
     for h in range(2):
         across_a(h)
-    w_step(1)
+    w_beats(6)
     for h in range(2):
         forward_b(h, -1)
-    w_step(2)
+    w_beats(2)
     for h in range(2):
         forward_b(h, 1)
-    w_step(3)
+    w_beats(3)
     for h in range(2):
         across_b(h, 0)
-
-    @pl.when(native)
-    def _():
-        w_copy.wait()
+    w_beats(5)
+    for h in range(2):
+        forward_b(h, 2)
+    w_beats(2)
 
     slab = sz.columns
 
     def turn(j, carry):
         first = pl.multiple_of(j * slab, slab)
-        w_t[:, pl.ds(first, slab)] = w_buf[pl.ds(first, slab), :].T
+        for half in range(Z_HI):
+            w_t[half * sz.share : (half + 1) * sz.share, pl.ds(first, slab)] = w_buf[half, pl.ds(first, slab), :].T
         return carry
 
     lax.fori_loop(0, sz.features // slab, turn, 0)
     two_tiles(0)
-    for h in range(2):
-        forward_b(h, 2)
     two_tiles(1)
-    two_tiles(-1)
     for h in range(2):
         across_b(h, -1)
         across_b(h, 1)
+    two_tiles(-1)
     for h in range(2):
         across_b(h, 2)
     two_tiles(2)
@@ -304,7 +326,8 @@
 
     def probs_tile(t, carry):
         scaled = expd[t] * factor[pl.ds(t, 1), :]
-        column = lax.broadcasted_iota(jnp.int32, (sz.columns, sz.tile), 0)
+        row = lax.broadcasted_iota(jnp.int32, (Z_HI * sz.share, sz.tile), 0)
+        column = jnp.where(row < sz.share, row, row + PLANE * sz.columns - sz.share)
         lanes = pl.ds(pl.multiple_of(t * sz.tile, sz.tile), sz.tile)
         for d, labels in enumerate((tgt, smp)):
             hit = column == labels[pl.ds(t, 1), :]
@@ -313,7 +336,7 @@
 
     lax.fori_loop(0, TILES, probs_tile, 0)
 
-    sub = sz.columns // 2
+    sub = sz.share // RING_PARTS
 
     def rs_copy(d, slot, u):
         block = ring.at[d, slot, u]
@@ -322,76 +345,65 @@
             device_id=device(dz=1 if d == 0 else NZ - 1), device_id_type=MESH,
         )
 
-    def product(d, quarter):
-        lanes = pl.ds(pl.multiple_of(quarter * sz.quarter, sz.quarter), sz.quarter)
-        part_sum[d] = jnp.dot(probs[d], normed[:, lanes], preferred_element_type=F32)
-
     def owner(d, k):
         return (z + NZ - 1 - k) % NZ if d == 0 else (z + 1 + k) % NZ
 
+    def product(d, k):
+        to = owner(d, k)
+        rows = pl.ds(pl.multiple_of(to // Z_LO * sz.share, sz.share), sz.share)
+        lanes = pl.ds(pl.multiple_of(to % Z_LO * sz.quarter, sz.quarter), sz.quarter)
+        part_sum[k % 2, d] = jnp.dot(probs[d, rows, :], normed[:, lanes], preferred_element_type=F32)
+
+    def piece(d, k, u):
+        rows = slice(u * sub, (u + 1) * sub)
+        slot = owner(d, k)
+
+        @pl.when(k == 0)
+        def _():
+            ring[d, slot, u] = part_sum[k % 2, d, rows, :].astype(BF16)
+
+        @pl.when(k > 0)
+        def _():
+            rs_copy(d, slot, u).wait_recv()
+            ring[d, slot, u] = (ring[d, slot, u].astype(F32) + part_sum[k % 2, d, rows, :]).astype(BF16)
+
+        rs_copy(d, slot, u).start()
+
+    for d in range(2):
+        product(d, 0)
+
     def hop(k, carry):
-        for d in range(2):
-            to = owner(d, k)
-
-            @pl.when(to // Z_LO == core)
-            def _():
-                product(d, to % Z_LO)
-
-        for d in range(2):
-            to = owner(d, k)
-
-            @pl.when(to // Z_LO == core)
-            def _():
-                slot = to % Z_LO
-                for u in range(2):
-                    rows = slice(u * sub, (u + 1) * sub)
-
-                    @pl.when(k == 0)
-                    def _():
-                        ring[d, slot, u] = part_sum[d, rows, :].astype(BF16)
-
-                    @pl.when(k > 0)
-                    def _():
-                        rs_copy(d, slot, u).wait_recv()
-                        ring[d, slot, u] = (ring[d, slot, u].astype(F32) + part_sum[d, rows, :]).astype(BF16)
-
-                    rs_copy(d, slot, u).start()
-
+        for u in range(RING_PARTS):
+            for d in range(2):
+                piece(d, k, u)
+            if u < 2:
+                product(u, k + 1)
         return carry
 
     lax.fori_loop(0, NZ - 1, hop, 0)
 
-    def fin_copy(cc):
-        rows = pl.ds(pl.multiple_of(cc * sz.state_rows, sz.state_rows), sz.state_rows)
+    def fin_copy(d):
+        rows = pl.ds(pl.multiple_of((1 - core) * sz.state_rows, sz.state_rows), sz.state_rows)
         return pltpu.make_async_remote_copy(
-            src_ref=totals.at[:, rows], dst_ref=mine_out, send_sem=fin_send, recv_sem=fin_recv,
+            src_ref=totals.at[d, rows], dst_ref=other.at[d], send_sem=fin_send.at[d], recv_sem=fin_recv.at[d],
             device_id=device(dc=1), device_id_type=MESH,
         )
 
-    @pl.when(native)
-    def _():
-        for d in range(2):
-            product(d, z_lo)
-        for d in range(2):
-            for u in range(2):
-                rows = slice(u * sub, (u + 1) * sub)
-                rs_copy(d, z_lo, u).wait_recv()
-                total = ring[d, z_lo, u].astype(F32) + part_sum[d, rows, :]
-                totals[d, :, rows] = total.T.astype(BF16)
-        fin_copy(1 - core).start()
-        own = pl.ds(pl.multiple_of(core * sz.state_rows, sz.state_rows), sz.state_rows)
-        mine_out[...] = totals[:, own, :]
-
-    @pl.when(jnp.logical_not(native))
-    def _():
-        fin_copy(0).wait_recv()
-
-    gradient, sample_grad = mine_out[0].astype(F32), mine_out[1].astype(F32)
-    moment_new = BETA_ONE * moment[...].astype(F32) + (1.0 - BETA_ONE) * gradient
-    curvature_new = BETA_TWO * curvature[...].astype(F32) + (1.0 - BETA_TWO) * sample_grad * sample_grad
-    moment_out[...] = moment_new.astype(BF16)
-    curvature_out[...] = curvature_new.astype(BF16)
-    update_out[...] = jnp.clip(moment_new / (RHO_SCALE * curvature_new), -1.0, 1.0).astype(BF16)
+    own = pl.ds(pl.multiple_of(core * sz.state_rows, sz.state_rows), sz.state_rows)
+    for d in range(2):
+        for first in range(0, sz.share, 128):
+            rows = slice(first, first + 128)
+            for u in range(first // sub, (first + 128) // sub):
+                rs_copy(d, z, u).wait_recv()
+            block = ring[d, z, first // sub : (first + 128) // sub].reshape(128, sz.quarter)
+            total = block.astype(F32) + part_sum[(NZ - 1) % 2, d, rows, :]
+            totals[d, :, rows] = total.T.astype(BF16)
+        start(fin_copy(d))
+        mine_out[d, :, share] = totals[d, own, :]
+    others = pl.ds(pl.multiple_of((1 - core) * sz.share, sz.share), sz.share)
+    for d in range(2):
+        fin_copy(d).wait_recv()
+        mine_out[d, :, others] = other[d]
 
     for copy in sent:
         copy.wait_send()
@@ -399,20 +411,11 @@
 
     def drain(k, carry):
         for d in range(2):
-            to = owner(d, k)
-
-            @pl.when(to // Z_LO == core)
-            def _():
-                for u in range(2):
-                    rs_copy(d, to % Z_LO, u).wait_send()
-
+            for u in range(RING_PARTS):
+                rs_copy(d, owner(d, k), u).wait_send()
         return carry
 
     lax.fori_loop(0, NZ - 1, drain, 0)
-
-    @pl.when(native)
-    def _():
-        fin_copy(0).wait_send()
 
 
 def plane_labels(input_ids, sampled_ids, columns):
@@ -421,7 +424,7 @@
     tokens = input_ids.shape[0]
     span = tokens // (NZ * CORES)
     group = tokens // (Z_LO * CORES)
-    first_col = (core * PLANE + place) * columns
+    first_col = place * columns + core * (columns // CORES)
     position = jnp.arange(tokens)
     targets = jnp.where(position % group < group - 1, jnp.roll(input_ids, -1), -1)
 
@@ -442,24 +445,23 @@
     sz = Sizes(rows, features, columns, moment.shape[0])
     tgt, smp = plane_labels(input_ids, sampled_ids, columns)
     vmem = pl.BlockSpec(memory_space=pltpu.VMEM)
-    state = jax.ShapeDtypeStruct(moment.shape, BF16)
     dma = pltpu.SemaphoreType.DMA
     n_chunks = sz.weight_chunks // 2
-    return pl.pallas_call(
+    sums = pl.pallas_call(
         lambda *refs: kernel(sz, *refs),
-        out_shape=(state, state, state),
-        in_specs=[vmem, vmem, vmem, vmem, pl.BlockSpec(memory_space=pl.ANY), vmem, vmem],
-        out_specs=(vmem, vmem, vmem),
+        out_shape=jax.ShapeDtypeStruct((2, *moment.shape), BF16),
+        in_specs=[vmem, vmem, vmem, vmem, pl.BlockSpec(memory_space=pl.ANY)],
+        out_specs=vmem,
         scratch_shapes=[
             pltpu.VMEM((sz.tokens, features), BF16),
-            pltpu.VMEM((features, columns), BF16),
+            pltpu.VMEM((Z_HI, features, sz.share), BF16),
             pltpu.VMEM((columns, features), BF16),
             pltpu.VMEM((TILES, columns, sz.tile), F32),
             pltpu.VMEM((2, columns, sz.tokens), BF16),
-            pltpu.VMEM((2, Z_LO, 2, columns // 2, sz.quarter), BF16),
-            pltpu.VMEM((2, columns, sz.quarter), F32),
-            pltpu.VMEM((2, sz.quarter, columns), BF16),
-            pltpu.VMEM((2, sz.state_rows, columns), BF16),
+            pltpu.VMEM((2, NZ, RING_PARTS, sz.share // RING_PARTS, sz.quarter), BF16),
+            pltpu.VMEM((2, 2, sz.share, sz.quarter), F32),
+            pltpu.VMEM((2, sz.quarter, sz.share), BF16),
+            pltpu.VMEM((2, sz.state_rows, sz.share), BF16),
             pltpu.VMEM((2 * TILES, sz.tile), F32),
             pltpu.VMEM((7, 2 * TILES, sz.tile), F32),
             pltpu.VMEM((2 * TILES, sz.tile), F32),
@@ -476,15 +478,20 @@
             dma((7,)),
             dma((3,)),
             dma((3,)),
-            dma((2, Z_LO, 2)),
-            dma((2, Z_LO, 2)),
-            dma,
-            dma,
+            dma((2, NZ, RING_PARTS)),
+            dma((2, NZ, RING_PARTS)),
+            dma((2,)),
+            dma((2,)),
         ],
         compiler_params=pltpu.CompilerParams(
             collective_id=0, has_side_effects=True, vmem_limit_bytes=60 * 1024 * 1024
         ),
-    )(hidden, norm_gain.reshape(1, -1), tgt, smp, head_weight, moment, curvature)
+    )(hidden, norm_gain.reshape(1, -1), tgt, smp, head_weight)
+    gradient, sample_grad = sums[0].astype(F32), sums[1].astype(F32)
+    moment_new = BETA_ONE * moment.astype(F32) + (1.0 - BETA_ONE) * gradient
+    curvature_new = BETA_TWO * curvature.astype(F32) + (1.0 - BETA_TWO) * sample_grad * sample_grad
+    update_direction = jnp.clip(moment_new / (RHO_SCALE * curvature_new), -1.0, 1.0)
+    return moment_new.astype(BF16), curvature_new.astype(BF16), update_direction.astype(BF16)
 
 
 def solution(mesh):

time: 330 us -> 167 us (0.51)
  Pallas kernels: 316 us -> 156 us
  local copies, waits for them, and re-layouts: 11.5 us -> 6.14 us
    pallas_call x1, Pallas kernels: 316 us -> 156 us  [on_device(): pl.pallas_call(lambda *refs: kernel(sz, *refs), out_shape=jax.ShapeDtypeS...]
    unnamed x7 -> x8, local copies, waits for them, and re-layouts: 5.47 us -> 0.03 us
where the time goes in v2:
time: 167 us; the launch traced here: 166 us
  Pallas kernels  156 us (93%)
  local copies, waits for them, and re-layouts  6.14 us (4%)
  other arithmetic  3.58 us (2%)
    pallas_call x1, Pallas kernels, on_device(): pl.pallas_call(lambda *refs: kernel(sz, *refs), out_shape=jax.ShapeDtypeS...  156 us

profile of v2, /device:TPU:1, one launch (start us, length us, event | category | flops | bytes accessed | tf_op | source)
XLA Modules:
  0.0 166.4 jit_solution(15806008821495053671)
XLA Ops:
  0.6 0.0 copy-start.1
  0.6 0.0 copy-start
  0.7 1.3 slice.27
  2.0 1.3 reshape.32.refs_1_
  3.3 0.9 reshape.34
  4.2 0.9 slice.26
  5.1 0.7 pad_add_fusion
  5.9 0.1 fusion.5
  6.0 0.1 dynamic-slice_reduce_fusion
  6.1 0.1 reshape.35
  6.3 0.7 sub.27.refs_3_
  7.0 0.1 reshape.33
  7.2 0.7 sub.25.refs_2_
  7.9 155.9 %shard_map.94 = bf16[2,448,512]{2,1,0:T(8,128)(2,1)} custom-call(bf16[64,3584]{1,0:T(8,128)(2,1)} %refs_0_.1, f32[1,3584]{1,0:T(1,128)} %reshape.32.refs_1_, s32[8,256]{1,0:T(8,128)} %sub.25.refs_2_, s32[8,256]{1,0:T(8,128)} %sub.27.refs_3_, bf16[3584,512]{1,0:T(8,128)(2,1)} %refs_4_.1), custom_call_target="tpu_custom_call" | custom-call | tf_op jit(solution)/shard_map/pallas_call | solution.py:450
  163.8 0.0 copy-done.1
  163.8 0.0 copy-done
  163.8 2.6 %clamp_convert_fusion = (bf16[448,512]{1,0:T(8,128)(2,1)}, bf16[448,512]{1,0:T(8,128)(2,1)}, bf16[448,512]{1,0:T(8,128)(2,1)}) fusion(bf16[448,512]{1,0:T(8,128)(2,1)S(1)} %copy-done, bf16[448,512]{1,0:T(8,128)(2,1)S(1)} %copy-done.1, bf16[2,448,512]{2,1,0:T(8,128)(2,1)} %shard_map.94), kind=kLoop, calls=%fused_computation.3 | loop fusion | flops 3899392 | bytes 3211264 | tf_op jit(solution)/shard_map/convert_element_type | solution.py:494
  (13 shorter events, 0.3 us)
Async XLA Ops:
  0.6 163.2 %copy-start.1 = (bf16[448,512]{1,0:T(8,128)(2,1)S(1)}, bf16[448,512]{1,0:T(8,128)(2,1)}, u32[]{:S(2)}) copy-start(bf16[448,512]{1,0:T(8,128)(2,1)} %param.13) | copy-start | bytes 1376260
  0.6 163.2 %copy-start = (bf16[448,512]{1,0:T(8,128)(2,1)S(1)}, bf16[448,512]{1,0:T(8,128)(2,1)}, u32[]{:S(2)}) copy-start(bf16[448,512]{1,0:T(8,128)(2,1)} %param.12) | copy-start | bytes 1376260

commit v3 on v2

--- a/solution.py
+++ b/solution.py
@@ -14,7 +14,7 @@
 Z_LO, Z_HI, CORES = 4, 2, 2
 NZ = Z_HI * Z_LO
 PLANE = NX * NY
-W_SLACK = 3
+W_SLACK = 2
 W_AHEAD = 4
 RING_PARTS = 4
 TILES = 2 * 4
@@ -34,13 +34,13 @@
         self.tokens = TILES * self.tile
         self.state_rows = state_rows
         self.quarter = CORES * state_rows
-        self.weight_chunks = 32
+        self.weight_chunks = 16
 
 
 def kernel(
-    sz, hidden, gain, tgt, smp, weight, mine_out,
+    sz, hidden, gain, input_ids, sampled_ids, weight, mine_out,
     normed, w_buf, w_t, expd, probs, ring, part_sum, totals, other,
-    st_own, st_one, st_mid, st_two, factor,
+    st_own, st_one, st_mid, st_two, factor, labels,
     ag_send, ag_recv, sib_send, sib_recv, w_send, w_recv, w_local, s1_send, s1_recv, s2_send, s2_recv,
     rs_send, rs_recv, fin_send, fin_recv,
 ):
@@ -179,6 +179,34 @@
                 else:
                     w_copy_of(way, j, z_hi).wait_send()
 
+    def find_labels():
+        lanes = input_ids.shape[1]
+        span = NX * NY * sz.rows // lanes
+        first_col = (shard % PLANE) * sz.columns + core * sz.share
+        row = lax.broadcasted_iota(jnp.int32, (span, lanes), 0)
+        lane = lax.broadcasted_iota(jnp.int32, (span, lanes), 1)
+        found = [[], []]
+        for cc in range(CORES):
+            block = (z_lo * CORES + cc) * Z_HI + z_hi
+            now = pl.ds(pl.multiple_of(block * span, span), span)
+            later = pl.ds(pl.multiple_of((block + 1) % (NZ * CORES) * span, span), span)
+            ids = input_ids[now, :]
+            up = jnp.concatenate([ids[1:], input_ids[later, :][:1]], axis=0)
+            following = jnp.where(lane == lanes - 1, pltpu.roll(up, lanes - 1, 1), pltpu.roll(ids, lanes - 1, 1))
+            last = (z_hi == Z_HI - 1) & (row == span - 1) & (lane == lanes - 1)
+            found[0].append(jnp.where(last, -1, following) - first_col)
+            found[1].append(sampled_ids[now, :] - first_col)
+        for d in range(2):
+            for h in range(2):
+                for b in range(4):
+                    pieces = []
+                    for a in range(4):
+                        xx, yy = (a, b) if h == 0 else (b, a)
+                        at = (xx * NY + yy) * sz.rows + h * sz.half
+                        for cc in range(CORES):
+                            pieces.append(found[d][cc][at // lanes : at // lanes + 1, at % lanes : at % lanes + sz.half])
+                    labels[d, h * 4 + b : h * 4 + b + 1, :] = jnp.concatenate(pieces, axis=1)
+
     def logits_tile(t):
         rows = pl.ds(pl.multiple_of(t * sz.tile, sz.tile), sz.tile)
         logits = lax.dot_general(
@@ -243,37 +271,38 @@
         for _ in range(many):
             w_step(next(beats))
 
+    slab = sz.columns
+
+    def turn(half):
+        def body(j, carry):
+            first = pl.multiple_of(j * slab, slab)
+            rows = pl.ds(pl.multiple_of(half * sz.share, sz.share), sz.share)
+            w_t[rows, pl.ds(first, slab)] = w_buf[half, pl.ds(first, slab), :].T
+            return carry
+
+        lax.fori_loop(0, sz.features // slab, body, 0)
+
+    turn(z_hi)
     w_beats(3)
     for h in range(2):
         forward_a(h)
+    find_labels()
     w_beats(4)
     for h in range(2):
         forward_b(h, 0)
     for h in range(2):
         across_a(h)
-    w_beats(6)
+    w_beats(3)
     for h in range(2):
         forward_b(h, -1)
-    w_beats(2)
-    for h in range(2):
         forward_b(h, 1)
+    for h in range(2):
+        across_b(h, 0)
     w_beats(3)
     for h in range(2):
-        across_b(h, 0)
-    w_beats(5)
-    for h in range(2):
         forward_b(h, 2)
-    w_beats(2)
-
-    slab = sz.columns
-
-    def turn(j, carry):
-        first = pl.multiple_of(j * slab, slab)
-        for half in range(Z_HI):
-            w_t[half * sz.share : (half + 1) * sz.share, pl.ds(first, slab)] = w_buf[half, pl.ds(first, slab), :].T
-        return carry
-
-    lax.fori_loop(0, sz.features // slab, turn, 0)
+    w_beats(1)
+    turn(1 - z_hi)
     two_tiles(0)
     two_tiles(1)
     for h in range(2):
@@ -329,8 +358,8 @@
         row = lax.broadcasted_iota(jnp.int32, (Z_HI * sz.share, sz.tile), 0)
         column = jnp.where(row < sz.share, row, row + PLANE * sz.columns - sz.share)
         lanes = pl.ds(pl.multiple_of(t * sz.tile, sz.tile), sz.tile)
-        for d, labels in enumerate((tgt, smp)):
-            hit = column == labels[pl.ds(t, 1), :]
+        for d in range(2):
+            hit = column == labels[d, pl.ds(t, 1), :]
             probs[d, :, lanes] = jnp.where(hit, scaled - 1.0, scaled).astype(BF16)
         return carry
 
@@ -418,32 +447,11 @@
     lax.fori_loop(0, NZ - 1, drain, 0)
 
 
-def plane_labels(input_ids, sampled_ids, columns):
-    rep, shard = lax.axis_index("rep"), lax.axis_index("shard")
-    z_lo, core, z_hi, place = rep // CORES, rep % CORES, shard // PLANE, shard % PLANE
-    tokens = input_ids.shape[0]
-    span = tokens // (NZ * CORES)
-    group = tokens // (Z_LO * CORES)
-    first_col = place * columns + core * (columns // CORES)
-    position = jnp.arange(tokens)
-    targets = jnp.where(position % group < group - 1, jnp.roll(input_ids, -1), -1)
-
-    def of_plane(ids):
-        mine = ids.reshape(Z_LO, CORES, Z_HI, span)
-        mine = lax.dynamic_slice(mine, (z_lo, 0, z_hi, 0), (1, CORES, 1, span))
-        mine = mine.reshape(CORES, NX, NY, 2, -1)
-        first = mine[:, :, :, 0].transpose(2, 1, 0, 3)
-        second = mine[:, :, :, 1].transpose(1, 2, 0, 3)
-        return jnp.concatenate([first, second]).reshape(TILES, -1)
-
-    return of_plane(targets) - first_col, of_plane(sampled_ids) - first_col
-
-
 def on_device(hidden, norm_gain, input_ids, sampled_ids, head_weight, moment, curvature):
     rows, features = hidden.shape
     columns = head_weight.shape[1]
     sz = Sizes(rows, features, columns, moment.shape[0])
-    tgt, smp = plane_labels(input_ids, sampled_ids, columns)
+    lanes = 128
     vmem = pl.BlockSpec(memory_space=pltpu.VMEM)
     dma = pltpu.SemaphoreType.DMA
     n_chunks = sz.weight_chunks // 2
@@ -467,6 +475,7 @@
             pltpu.VMEM((2 * TILES, sz.tile), F32),
             pltpu.VMEM((3, 2 * TILES, sz.tile), F32),
             pltpu.VMEM((TILES, sz.tile), F32),
+            pltpu.VMEM((2, TILES, sz.tile), jnp.int32),
             dma((2, 20)),
             dma((2, 4, 4, 2)),
             dma((2, 16)),
@@ -486,7 +495,7 @@
         compiler_params=pltpu.CompilerParams(
             collective_id=0, has_side_effects=True, vmem_limit_bytes=60 * 1024 * 1024
         ),
-    )(hidden, norm_gain.reshape(1, -1), tgt, smp, head_weight)
+    )(hidden, norm_gain.reshape(1, -1), input_ids.reshape(-1, lanes), sampled_ids.reshape(-1, lanes), head_weight)
     gradient, sample_grad = sums[0].astype(F32), sums[1].astype(F32)
     moment_new = BETA_ONE * moment.astype(F32) + (1.0 - BETA_ONE) * gradient
     curvature_new = BETA_TWO * curvature.astype(F32) + (1.0 - BETA_TWO) * sample_grad * sample_grad

time: 167 us -> 153 us (0.916)
  Pallas kernels: 156 us -> 149 us
  local copies, waits for them, and re-layouts: 6.14 us -> 1.41 us
    pallas_call x1, Pallas kernels: 156 us -> 149 us  [on_device(): pl.pallas_call(lambda *refs: kernel(sz, *refs), out_shape=jax.ShapeDtypeS...]
    slice x4 -> x0, local copies, waits for them, and re-layouts: 2.24 us -> none  [the longest x2 2.19 us: plane_labels(): jnp.roll(input_ids, -1)]
where the time goes in v3:
time: 153 us
  Pallas kernels  149 us (97%)
  other arithmetic  2.58 us (2%)
    pallas_call x1, Pallas kernels, on_device(): pl.pallas_call(lambda *refs: kernel(sz, *refs), out_shape=jax.ShapeDtypeS...  149 us

profile of v3, /device:TPU:1, one launch (start us, length us, event | category | flops | bytes accessed | tf_op | source)
XLA Modules:
  0.0 153.3 jit_solution(12212371668740658099)
XLA Ops:
  0.6 0.0 copy-start.1
  0.6 0.0 copy-start
  0.7 1.4 reshape.20.refs_1_
  2.1 148.6 %shard_map.94 = bf16[2,448,512]{2,1,0:T(8,128)(2,1)} custom-call(bf16[64,3584]{1,0:T(8,128)(2,1)} %refs_0_.1, f32[1,3584]{1,0:T(1,128)} %reshape.20.refs_1_, s32[128,128]{1,0:T(8,128)} %bitcast.12, s32[128,128]{1,0:T(8,128)} %bitcast.13, bf16[3584,512]{1,0:T(8,128)(2,1)} %refs_4_.1), custom_call_target="tpu_custom_call" | custom-call | tf_op jit(solution)/shard_map/pallas_call | solution.py:458
  150.7 0.0 copy-done.1
  150.7 0.0 copy-done
  150.7 2.6 %clamp_convert_fusion = (bf16[448,512]{1,0:T(8,128)(2,1)}, bf16[448,512]{1,0:T(8,128)(2,1)}, bf16[448,512]{1,0:T(8,128)(2,1)}) fusion(bf16[448,512]{1,0:T(8,128)(2,1)S(1)} %copy-done, bf16[448,512]{1,0:T(8,128)(2,1)S(1)} %copy-done.1, bf16[2,448,512]{2,1,0:T(8,128)(2,1)} %shard_map.94), kind=kLoop, calls=%fused_computation.3 | loop fusion | flops 3899392 | bytes 3211264 | tf_op jit(solution)/shard_map/convert_element_type | solution.py:503
Async XLA Ops:
  0.6 150.1 %copy-start.1 = (bf16[448,512]{1,0:T(8,128)(2,1)S(1)}, bf16[448,512]{1,0:T(8,128)(2,1)}, u32[]{:S(2)}) copy-start(bf16[448,512]{1,0:T(8,128)(2,1)} %param.13) | copy-start | bytes 1376260
  0.6 150.1 %copy-start = (bf16[448,512]{1,0:T(8,128)(2,1)S(1)}, bf16[448,512]{1,0:T(8,128)(2,1)}, u32[]{:S(2)}) copy-start(bf16[448,512]{1,0:T(8,128)(2,1)} %param.12) | copy-start | bytes 1376260

commit v4 on v3

--- a/solution.py
+++ b/solution.py
@@ -16,7 +16,7 @@
 PLANE = NX * NY
 W_SLACK = 2
 W_AHEAD = 4
-RING_PARTS = 4
+RING_PARTS = 2
 TILES = 2 * 4
 BF16, F32 = jnp.bfloat16, jnp.float32
 MESH = pl.DeviceIdType.MESH
@@ -35,14 +35,20 @@
         self.state_rows = state_rows
         self.quarter = CORES * state_rows
         self.weight_chunks = 16
+        self.wide = 256
+        self.middle = self.quarter - 2 * self.wide
+        self.lanes = self.quarter + self.middle
+        self.far_block = NZ // 2 * CORES * rows
+        self.far_tokens = 2 * PLANE * self.far_block
 
 
 def kernel(
     sz, hidden, gain, input_ids, sampled_ids, weight, mine_out,
-    normed, w_buf, w_t, expd, probs, ring, part_sum, totals, other,
+    normed, w_buf, w_t, expd, probs, plain, ring, part_sum, totals, other, other_sample,
+    own_rows, far, far_sum, far_turned, far_labels,
     st_own, st_one, st_mid, st_two, factor, labels,
     ag_send, ag_recv, sib_send, sib_recv, w_send, w_recv, w_local, s1_send, s1_recv, s2_send, s2_recv,
-    rs_send, rs_recv, fin_send, fin_recv,
+    rs_send, rs_recv, fin_send, fin_recv, x_send, x_recv, f_send, f_recv,
 ):
     rep, shard = lax.axis_index("rep"), lax.axis_index("shard")
     z_lo, core = rep // CORES, rep % CORES
@@ -58,7 +64,7 @@
     barrier = pltpu.get_barrier_semaphore()
     partners = [device(dx=dx, dc=dc) for dx, dc in row_peers]
     partners += [device(dy=dy) for dy in column_peers]
-    partners += [device(dz=1), device(dz=NZ - 1)]
+    partners += [device(dz=dz, dc=dc) for dz in range(1, NZ) for dc in range(CORES)]
     for partner in partners:
         pl.semaphore_signal(barrier, inc=1, device_id=partner, device_id_type=MESH)
 
@@ -74,7 +80,10 @@
         values = hidden[pl.ds(h * sz.half, sz.half), :].astype(F32)
         scale = lax.rsqrt(jnp.mean(values * values, axis=-1, keepdims=True) + EPS_NORM)
         rows = pl.ds(pl.multiple_of(block_row(h, 0, 0, core), sz.half), sz.half)
-        normed[rows, :] = (values * scale * gain[...]).astype(BF16)
+        block = (values * scale * gain[...]).astype(BF16)
+        normed[rows, :] = block
+        own_rows[h * sz.half : (h + 1) * sz.half, :] = block
+    far_sum[...] = jnp.zeros_like(far_sum)
     pl.semaphore_wait(barrier, len(partners))
 
     sent = []
@@ -83,40 +92,76 @@
         copy.start()
         sent.append(copy)
 
-    def ag_copy(h, da, db, part, along, step, index):
-        to_a, to_b = (step, 0) if along == 0 else (0, step)
-        dx, dy = (to_a, to_b) if h == 0 else (to_b, to_a)
-        first = block_row(h, da, db, core)
-        if part is None:
-            rows = pl.ds(pl.multiple_of(first, sz.half), sz.half)
-        else:
-            rows = pl.ds(pl.multiple_of(first + part * sz.part, sz.part), sz.part)
-        block = normed.at[rows]
-        return pltpu.make_async_remote_copy(
-            src_ref=block, dst_ref=block, send_sem=ag_send.at[h, index],
-            recv_sem=ag_recv.at[h, (da - to_a) % 4, (db - to_b) % 4, part or 0],
-            device_id=device(dx=dx, dy=dy), device_id_type=MESH,
-        )
-
-    counts = [0, 0]
-
-    def ag_send_block(h, da, db, part, along, step):
-        start(ag_copy(h, da % 4, db % 4, part, along, step, counts[h]))
-        counts[h] += 1
-
-    def ag_wait(h, da, db):
-        da, db = da % 4, db % 4
-        first = block_row(h, da, db, core)
-        split = da == 2 if db == 0 else db == 2
-        for part in (0, 1) if split else (None,):
+    class Gather:
+        def __init__(self, buffer, first_row, size, send_sems, recv_sems, on_arrival):
+            self.buffer, self.first_row, self.size = buffer, first_row, size
+            self.send_sems, self.recv_sems, self.on_arrival = send_sems, recv_sems, on_arrival
+            self.sends = []
+
+        def block(self, h, da, db, part):
+            first = self.first_row(h, da, db)
             if part is None:
-                rows = pl.ds(pl.multiple_of(first, sz.half), sz.half)
-            else:
-                rows = pl.ds(pl.multiple_of(first + part * sz.part, sz.part), sz.part)
-            pltpu.make_async_remote_copy(
-                src_ref=normed.at[rows], dst_ref=normed.at[rows], send_sem=ag_send.at[h, 0],
-                recv_sem=ag_recv.at[h, da, db, part or 0], device_id=device(dx=1), device_id_type=MESH,
-            ).wait_recv()
+                return self.buffer.at[pl.ds(pl.multiple_of(first, self.size), self.size)]
+            size = self.size // 2
+            return self.buffer.at[pl.ds(pl.multiple_of(first + part * size, size), size)]
+
+        def copy(self, index, h, da, db, part, along, step):
+            to_a, to_b = (step, 0) if along == 0 else (0, step)
+            dx, dy = (to_a, to_b) if h == 0 else (to_b, to_a)
+            block = self.block(h, da, db, part)
+            return pltpu.make_async_remote_copy(
+                src_ref=block, dst_ref=block, send_sem=self.send_sems.at[index],
+                recv_sem=self.recv_sems.at[h, (da - to_a) % 4, (db - to_b) % 4, part or 0],
+                device_id=device(dx=dx, dy=dy), device_id_type=MESH,
+            )
+
+        def send(self, *what):
+            self.copy(len(self.sends), *what).start()
+            self.sends.append(what)
+
+        def wait_sends(self):
+            for index, what in enumerate(self.sends):
+                self.copy(index, *what).wait_send()
+
+        def wait(self, h, da, db):
+            split = da % 4 == 2 if db % 4 == 0 else db % 4 == 2
+            for part in (0, 1) if split else (None,):
+                block = self.block(h, da, db, part)
+                pltpu.make_async_remote_copy(
+                    src_ref=block, dst_ref=block, send_sem=self.send_sems.at[0],
+                    recv_sem=self.recv_sems.at[h, da % 4, db % 4, part or 0],
+                    device_id=device(dx=1), device_id_type=MESH,
+                ).wait_recv()
+
+        def begin(self, along):
+            for h in range(2):
+                for step in (1, -1):
+                    self.send(h, 0, 0, None, along, step)
+
+        def forward_a(self, h):
+            for da in (-1, 1):
+                self.wait(h, da, 0)
+                self.send(h, da, 0, 0 if da == -1 else 1, 0, -da)
+            for da in (-1, 1):
+                for step in (1, -1):
+                    self.send(h, da, 0, None, 1, step)
+                self.on_arrival(h, da, 0)
+
+        def across_a(self, h):
+            self.wait(h, 2, 0)
+            for step in (1, -1):
+                self.send(h, 2, 0, None, 1, step)
+            self.on_arrival(h, 2, 0)
+
+        def forward_b(self, h, da):
+            for db in (-1, 1):
+                self.wait(h, da, db)
+                self.send(h, da, db, 0 if db == -1 else 1, 1, -db)
+                self.on_arrival(h, da, db)
+
+        def across_b(self, h, da):
+            self.wait(h, da, 2)
+            self.on_arrival(h, da, 2)
 
     def sib_copy(h, da, db, cc):
         rows = pl.ds(pl.multiple_of(block_row(h, da, db, cc), sz.half), sz.half)
@@ -229,41 +274,13 @@
 
         lax.fori_loop(0, 2, body, 0)
 
-    for h in range(2):
-        for step in (1, -1):
-            ag_send_block(h, 0, 0, None, 0, step)
-
+    near = Gather(normed, lambda h, da, db: block_row(h, da, db, core), sz.half, ag_send, ag_recv, to_sibling)
+    near.begin(0)
     w_copy.wait()
     w_first()
-    for h in range(2):
-        for step in (1, -1):
-            ag_send_block(h, 0, 0, None, 1, step)
+    near.begin(1)
+    for h in range(2):
         to_sibling(h, 0, 0)
-
-    def forward_a(h):
-        for da in (-1, 1):
-            ag_wait(h, da, 0)
-            ag_send_block(h, da, 0, 0 if da == -1 else 1, 0, -da)
-        for da in (-1, 1):
-            for step in (1, -1):
-                ag_send_block(h, da, 0, None, 1, step)
-            to_sibling(h, da, 0)
-
-    def across_a(h):
-        ag_wait(h, 2, 0)
-        for step in (1, -1):
-            ag_send_block(h, 2, 0, None, 1, step)
-        to_sibling(h, 2, 0)
-
-    def forward_b(h, da):
-        for db in (-1, 1):
-            ag_wait(h, da, db)
-            ag_send_block(h, da, db, 0 if db == -1 else 1, 1, -db)
-            to_sibling(h, da, db)
-
-    def across_b(h, da):
-        ag_wait(h, da, 2)
-        to_sibling(h, da, 2)
 
     beats = iter(range(up_chunks + W_SLACK * (Z_LO - 1)))
 
@@ -282,35 +299,104 @@
 
         lax.fori_loop(0, sz.features // slab, body, 0)
 
+    def far_row(h, da, db):
+        a, b = (x, y) if h == 0 else (y, x)
+        return ((h * 4 + (b + db) % 4) * 4 + (a + da) % 4) * sz.far_block
+
+    def far_lanes(dz, dc):
+        first = (z + dz) % NZ % Z_LO * sz.quarter + (core + dc) % CORES * (sz.quarter - sz.wide)
+        return pl.ds(pl.multiple_of(first, 128), sz.wide)
+
+    def far_own(zz, cc):
+        place = jnp.where(zz // Z_LO == 0, y * 4 + x, x * 4 + y)
+        first = (zz // Z_LO * PLANE + place) * sz.far_block + (zz % Z_LO * CORES + cc) * sz.rows
+        return pl.ds(pl.multiple_of(first, sz.rows), sz.rows)
+
+    offsets = [(dz, dc) for dz in range(NZ) for dc in range(CORES) if (dz, dc) != (0, 0)]
+
+    def exchange(dz, dc):
+        return pltpu.make_async_remote_copy(
+            src_ref=own_rows.at[:, far_lanes(dz, dc)], dst_ref=far.at[far_own(z, core)],
+            send_sem=x_send.at[dz, dc], recv_sem=x_recv.at[dz, dc],
+            device_id=device(dz=dz, dc=dc), device_id_type=MESH,
+        )
+
+    def exchange_start():
+        for dz, dc in offsets:
+            start(exchange(dz, dc))
+        far[far_own(z, core), :] = own_rows[:, far_lanes(0, 0)]
+
+    def exchange_wait():
+        for dz, dc in offsets:
+            exchange(dz, dc).wait_recv()
+
+    second = Gather(far, far_row, sz.far_block, f_send, f_recv, lambda h, da, db: None)
+
+    def find_far_labels():
+        lanes = input_ids.shape[1]
+        rows = input_ids.shape[0]
+        span = rows // (NZ * CORES)
+        ids = input_ids[...]
+        row = lax.broadcasted_iota(jnp.int32, (rows, lanes), 0)
+        lane = lax.broadcasted_iota(jnp.int32, (rows, lanes), 1)
+        up = jnp.concatenate([ids[1:], ids[:1]], axis=0)
+        following = jnp.where(lane == lanes - 1, pltpu.roll(up, lanes - 1, 1), pltpu.roll(ids, lanes - 1, 1))
+        last = (row % (Z_HI * span) == Z_HI * span - 1) & (lane == lanes - 1)
+        for d, found in enumerate((jnp.where(last, -1, following), sampled_ids[...])):
+            found = found - shard * sz.columns
+            for h in range(Z_HI):
+                for odd in range(2):
+                    pieces = []
+                    for rr in range(Z_LO * CORES):
+                        first = (rr * Z_HI + h) * span
+                        pieces.append(found[first : first + span, odd * sz.rows : (odd + 1) * sz.rows])
+                    far_labels[d, h, odd] = jnp.concatenate(pieces, axis=1)
+
+    def far_blocks(offset):
+        def body(i, carry):
+            h, a = i // 4, i % 4
+            b = (jnp.where(h == 0, y, x) + offset) % 4
+            rows = pl.ds(pl.multiple_of((i // 4 * PLANE + b * 4 + a) * sz.far_block, sz.far_block), sz.far_block)
+            place = jnp.where(h == 0, a * 4 + b, b * 4 + a)
+            column = lax.broadcasted_iota(jnp.int32, (sz.columns, sz.far_block), 0)
+            for d in range(2):
+                hit = column == far_labels[d, h, place % 2, pl.ds(place // 2, 1), :]
+                one_hot = jnp.where(hit, 1.0, 0.0).astype(BF16)
+                far_sum[d] += jnp.dot(one_hot, far[rows, :], preferred_element_type=F32)
+            return carry
+
+        lax.fori_loop(0, 8, body, 0)
+
     turn(z_hi)
     w_beats(3)
     for h in range(2):
-        forward_a(h)
+        near.forward_a(h)
     find_labels()
     w_beats(4)
     for h in range(2):
-        forward_b(h, 0)
-    for h in range(2):
-        across_a(h)
+        near.forward_b(h, 0)
+    for h in range(2):
+        near.across_a(h)
     w_beats(3)
     for h in range(2):
-        forward_b(h, -1)
-        forward_b(h, 1)
-    for h in range(2):
-        across_b(h, 0)
+        near.forward_b(h, -1)
+        near.forward_b(h, 1)
+    for h in range(2):
+        near.across_b(h, 0)
     w_beats(3)
     for h in range(2):
-        forward_b(h, 2)
+        near.forward_b(h, 2)
     w_beats(1)
+    exchange_start()
     turn(1 - z_hi)
     two_tiles(0)
     two_tiles(1)
     for h in range(2):
-        across_b(h, -1)
-        across_b(h, 1)
+        near.across_b(h, -1)
+        near.across_b(h, 1)
     two_tiles(-1)
     for h in range(2):
-        across_b(h, 2)
+        near.across_b(h, 2)
     two_tiles(2)
 
     def join(pairs):
@@ -348,6 +434,9 @@
     ]
     for copy in twos:
         start(copy)
+    exchange_wait()
+    second.begin(0)
+    second.begin(1)
     for copy in twos:
         copy.wait_recv()
     peak, total = join([pair(st_mid)] + [pair(st_two.at[j]) for j in range(len(column_peers))])
@@ -358,17 +447,21 @@
         row = lax.broadcasted_iota(jnp.int32, (Z_HI * sz.share, sz.tile), 0)
         column = jnp.where(row < sz.share, row, row + PLANE * sz.columns - sz.share)
         lanes = pl.ds(pl.multiple_of(t * sz.tile, sz.tile), sz.tile)
-        for d in range(2):
-            hit = column == labels[d, pl.ds(t, 1), :]
-            probs[d, :, lanes] = jnp.where(hit, scaled - 1.0, scaled).astype(BF16)
+        for half in range(Z_HI):
+            rows = slice(half * sz.share, (half + 1) * sz.share)
+            plain[half, :, lanes] = scaled[rows].astype(BF16)
+            for d in range(2):
+                less = jnp.where(column[rows] == labels[d, pl.ds(t, 1), :], scaled[rows] - 1.0, scaled[rows])
+                probs[half, d * sz.share : (d + 1) * sz.share, lanes] = less.astype(BF16)
         return carry
 
     lax.fori_loop(0, TILES, probs_tile, 0)
 
-    sub = sz.share // RING_PARTS
+    side = sz.share // 2
+    sub = side // RING_PARTS
 
     def rs_copy(d, slot, u):
-        block = ring.at[d, slot, u]
+        block = ring.at[slot, d, u]
         return pltpu.make_async_remote_copy(
             src_ref=block, dst_ref=block, send_sem=rs_send.at[d, slot, u], recv_sem=rs_recv.at[d, slot, u],
             device_id=device(dz=1 if d == 0 else NZ - 1), device_id_type=MESH,
@@ -377,63 +470,116 @@
     def owner(d, k):
         return (z + NZ - 1 - k) % NZ if d == 0 else (z + 1 + k) % NZ
 
-    def product(d, k):
-        to = owner(d, k)
-        rows = pl.ds(pl.multiple_of(to // Z_LO * sz.share, sz.share), sz.share)
-        lanes = pl.ds(pl.multiple_of(to % Z_LO * sz.quarter, sz.quarter), sz.quarter)
-        part_sum[k % 2, d] = jnp.dot(probs[d, rows, :], normed[:, lanes], preferred_element_type=F32)
+    def product(to):
+        half, first = to // Z_LO, to % Z_LO * sz.quarter
+        middle = normed[:, pl.ds(pl.multiple_of(first + sz.wide, 128), sz.middle)]
+        both = jnp.dot(probs[half], middle, preferred_element_type=F32).astype(BF16)
+        part_sum[to, :, sz.wide : sz.wide + sz.middle] = both[: sz.share]
+        part_sum[to, :, sz.quarter :] = both[sz.share :]
+        for at in (0, sz.quarter - sz.wide):
+            end = normed[:, pl.ds(pl.multiple_of(first + at, 128), sz.wide)]
+            part_sum[to, :, at : at + sz.wide] = jnp.dot(plain[half], end, preferred_element_type=F32).astype(BF16)
 
     def piece(d, k, u):
-        rows = slice(u * sub, (u + 1) * sub)
+        rows = slice(d * side + u * sub, d * side + (u + 1) * sub)
         slot = owner(d, k)
 
         @pl.when(k == 0)
         def _():
-            ring[d, slot, u] = part_sum[k % 2, d, rows, :].astype(BF16)
+            ring[slot, d, u] = part_sum[slot, rows, :]
 
         @pl.when(k > 0)
         def _():
             rs_copy(d, slot, u).wait_recv()
-            ring[d, slot, u] = (ring[d, slot, u].astype(F32) + part_sum[k % 2, d, rows, :]).astype(BF16)
+            ring[slot, d, u] = (ring[slot, d, u].astype(F32) + part_sum[slot, rows, :].astype(F32)).astype(BF16)
 
         rs_copy(d, slot, u).start()
 
     for d in range(2):
-        product(d, 0)
+        product(owner(d, 0))
+
+    def for_halves(act, *what):
+        for h in range(2):
+            act(h, *what)
+
+    beside = {
+        (0, 0): lambda: for_halves(second.forward_a),
+        (0, 1): find_far_labels,
+        (1, 0): lambda: for_halves(second.forward_b, 0),
+        (1, 1): lambda: for_halves(second.across_a),
+        (2, 0): lambda: far_blocks(0),
+        (2, 1): lambda: for_halves(second.forward_b, -1),
+        (3, 0): lambda: for_halves(second.forward_b, 1),
+        (3, 1): lambda: for_halves(second.across_b, 0),
+        (4, 0): lambda: for_halves(second.forward_b, 2),
+        (4, 1): lambda: far_blocks(1),
+        (5, 0): lambda: far_blocks(-1),
+        (5, 1): lambda: (for_halves(second.across_b, -1), for_halves(second.across_b, 1)),
+        (6, 0): lambda: for_halves(second.across_b, 2),
+        (6, 1): lambda: far_blocks(2),
+    }
 
     def hop(k, carry):
         for u in range(RING_PARTS):
             for d in range(2):
                 piece(d, k, u)
-            if u < 2:
-                product(u, k + 1)
+
+            @pl.when(k < 2)
+            def _():
+                product(owner(u, k + 1))
+
+            @pl.when(k == 2)
+            def _():
+                product(owner(0, 3) if u == 0 else z)
+
+            for step in range(NZ - 1):
+
+                @pl.when(k == step)
+                def _():
+                    beside[step, u]()
+
         return carry
 
     lax.fori_loop(0, NZ - 1, hop, 0)
 
-    def fin_copy(d):
-        rows = pl.ds(pl.multiple_of((1 - core) * sz.state_rows, sz.state_rows), sz.state_rows)
+    def fin_copy(i):
+        first, size, target = (
+            ((1 - core) * sz.state_rows, sz.state_rows, other),
+            (sz.quarter + (1 - core) * sz.middle // 2, sz.middle // 2, other_sample),
+        )[i]
         return pltpu.make_async_remote_copy(
-            src_ref=totals.at[d, rows], dst_ref=other.at[d], send_sem=fin_send.at[d], recv_sem=fin_recv.at[d],
-            device_id=device(dc=1), device_id_type=MESH,
-        )
-
-    own = pl.ds(pl.multiple_of(core * sz.state_rows, sz.state_rows), sz.state_rows)
+            src_ref=totals.at[pl.ds(pl.multiple_of(first, 64), size)], dst_ref=target, send_sem=fin_send.at[i],
+            recv_sem=fin_recv.at[i], device_id=device(dc=1), device_id_type=MESH,
+        )
+
     for d in range(2):
-        for first in range(0, sz.share, 128):
-            rows = slice(first, first + 128)
-            for u in range(first // sub, (first + 128) // sub):
-                rs_copy(d, z, u).wait_recv()
-            block = ring[d, z, first // sub : (first + 128) // sub].reshape(128, sz.quarter)
-            total = block.astype(F32) + part_sum[(NZ - 1) % 2, d, rows, :]
-            totals[d, :, rows] = total.T.astype(BF16)
-        start(fin_copy(d))
-        mine_out[d, :, share] = totals[d, own, :]
-    others = pl.ds(pl.multiple_of((1 - core) * sz.share, sz.share), sz.share)
+        far_turned[d] = far_sum[d].T
     for d in range(2):
-        fin_copy(d).wait_recv()
-        mine_out[d, :, others] = other[d]
-
+        for u in range(RING_PARTS):
+            rs_copy(d, z, u).wait_recv()
+        rows = slice(d * side, (d + 1) * side)
+        total = ring[z, d].reshape(side, sz.lanes).astype(F32) + part_sum[z, rows, :].astype(F32)
+        totals[:, rows] = total.T.astype(BF16)
+    for i in range(2):
+        start(fin_copy(i))
+    end_rows = pl.ds(pl.multiple_of(core * (sz.middle // 2), 64), sz.wide)
+    middle_rows = pl.ds(pl.multiple_of((1 - core) * sz.wide, 64), sz.middle // 2)
+
+    def place(sums, sampled, columns):
+        mine_out[0, middle_rows, columns] = sums[middle_rows, :]
+        mine_out[1, middle_rows, columns] = sampled[...]
+        for d in range(2):
+            mine_out[d, end_rows, columns] = (sums[end_rows, :].astype(F32) - far_turned[d, :, columns]).astype(BF16)
+
+    own_sums = totals.at[pl.ds(pl.multiple_of(core * sz.state_rows, 64), sz.state_rows)]
+    own_sample = totals.at[pl.ds(pl.multiple_of(sz.quarter + core * sz.middle // 2, 64), sz.middle // 2)]
+    place(own_sums, own_sample, share)
+    for i in range(2):
+        fin_copy(i).wait_recv()
+    place(other, other_sample, pl.ds(pl.multiple_of((1 - core) * sz.share, sz.share), sz.share))
+
+    near.wait_sends()
+    second.wait_sends()
     for copy in sent:
         copy.wait_send()
     w_finish()
@@ -465,18 +611,25 @@
             pltpu.VMEM((Z_HI, features, sz.share), BF16),
             pltpu.VMEM((columns, features), BF16),
             pltpu.VMEM((TILES, columns, sz.tile), F32),
-            pltpu.VMEM((2, columns, sz.tokens), BF16),
-            pltpu.VMEM((2, NZ, RING_PARTS, sz.share // RING_PARTS, sz.quarter), BF16),
-            pltpu.VMEM((2, 2, sz.share, sz.quarter), F32),
-            pltpu.VMEM((2, sz.quarter, sz.share), BF16),
-            pltpu.VMEM((2, sz.state_rows, sz.share), BF16),
+            pltpu.VMEM((Z_HI, 2 * sz.share, sz.tokens), BF16),
+            pltpu.VMEM((Z_HI, sz.share, sz.tokens), BF16),
+            pltpu.VMEM((NZ, 2, RING_PARTS, sz.share // 2 // RING_PARTS, sz.lanes), BF16),
+            pltpu.VMEM((NZ, sz.share, sz.lanes), BF16),
+            pltpu.VMEM((sz.lanes, sz.share), BF16),
+            pltpu.VMEM((sz.state_rows, sz.share), BF16),
+            pltpu.VMEM((sz.middle // 2, sz.share), BF16),
+            pltpu.VMEM((rows, features), BF16),
+            pltpu.VMEM((sz.far_tokens, sz.wide), BF16),
+            pltpu.VMEM((2, columns, sz.wide), F32),
+            pltpu.VMEM((2, sz.wide, columns), F32),
+            pltpu.VMEM((2, Z_HI, 2, PLANE // 2, sz.far_block), jnp.int32),
             pltpu.VMEM((2 * TILES, sz.tile), F32),
             pltpu.VMEM((7, 2 * TILES, sz.tile), F32),
             pltpu.VMEM((2 * TILES, sz.tile), F32),
             pltpu.VMEM((3, 2 * TILES, sz.tile), F32),
             pltpu.VMEM((TILES, sz.tile), F32),
             pltpu.VMEM((2, TILES, sz.tile), jnp.int32),
-            dma((2, 20)),
+            dma((40,)),
             dma((2, 4, 4, 2)),
             dma((2, 16)),
             dma((2, 16)),
@@ -491,6 +644,10 @@
             dma((2, NZ, RING_PARTS)),
             dma((2,)),
             dma((2,)),
+            dma((NZ, CORES)),
+            dma((NZ, CORES)),
+            dma((40,)),
+            dma((2, 4, 4, 2)),
         ],
         compiler_params=pltpu.CompilerParams(
             collective_id=0, has_side_effects=True, vmem_limit_bytes=60 * 1024 * 1024

time: 153 us -> 151 us (0.987)
  Pallas kernels: 149 us -> 146 us
    pallas_call x1, Pallas kernels: 149 us -> 146 us  [on_device(): pl.pallas_call(lambda *refs: kernel(sz, *refs), out_shape=jax.ShapeDtypeS...]
where the time goes in v4:
time: 151 us
  Pallas kernels  146 us (97%)
  other arithmetic  2.58 us (2%)
    pallas_call x1, Pallas kernels, on_device(): pl.pallas_call(lambda *refs: kernel(sz, *refs), out_shape=jax.ShapeDtypeS...  146 us

profile of v4, /device:TPU:1, one launch (start us, length us, event | category | flops | bytes accessed | tf_op | source)
XLA Modules:
  0.0 150.5 jit_solution(13275689736927192750)
XLA Ops:
  0.6 0.0 copy-start.1
  0.6 0.0 copy-start
  0.7 1.4 reshape.20.refs_1_
  2.1 145.9 %shard_map.94 = bf16[2,448,512]{2,1,0:T(8,128)(2,1)} custom-call(bf16[64,3584]{1,0:T(8,128)(2,1)} %refs_0_.1, f32[1,3584]{1,0:T(1,128)} %reshape.20.refs_1_, s32[128,128]{1,0:T(8,128)} %bitcast.12, s32[128,128]{1,0:T(8,128)} %bitcast.13, bf16[3584,512]{1,0:T(8,128)(2,1)} %refs_4_.1), custom_call_target="tpu_custom_call" | custom-call | tf_op jit(solution)/shard_map/pallas_call | solution.py:604
  147.9 0.0 copy-done.1
  148.0 0.0 copy-done
  148.0 2.6 %clamp_convert_fusion = (bf16[448,512]{1,0:T(8,128)(2,1)}, bf16[448,512]{1,0:T(8,128)(2,1)}, bf16[448,512]{1,0:T(8,128)(2,1)}) fusion(bf16[448,512]{1,0:T(8,128)(2,1)S(1)} %copy-done, bf16[448,512]{1,0:T(8,128)(2,1)S(1)} %copy-done.1, bf16[2,448,512]{2,1,0:T(8,128)(2,1)} %shard_map.94), kind=kLoop, calls=%fused_computation.3 | loop fusion | flops 3899392 | bytes 3211264 | tf_op jit(solution)/shard_map/convert_element_type | solution.py:660
Async XLA Ops:
  0.6 147.3 %copy-start.1 = (bf16[448,512]{1,0:T(8,128)(2,1)S(1)}, bf16[448,512]{1,0:T(8,128)(2,1)}, u32[]{:S(2)}) copy-start(bf16[448,512]{1,0:T(8,128)(2,1)} %param.13) | copy-start | bytes 1376260
  0.6 147.3 %copy-start = (bf16[448,512]{1,0:T(8,128)(2,1)S(1)}, bf16[448,512]{1,0:T(8,128)(2,1)}, u32[]{:S(2)}) copy-start(bf16[448,512]{1,0:T(8,128)(2,1)} %param.12) | copy-start | bytes 1376260

commit v5 on v4

--- a/solution.py
+++ b/solution.py
@@ -16,7 +16,7 @@
 PLANE = NX * NY
 W_SLACK = 2
 W_AHEAD = 4
-RING_PARTS = 2
+RING_PARTS = 4
 TILES = 2 * 4
 BF16, F32 = jnp.bfloat16, jnp.float32
 MESH = pl.DeviceIdType.MESH
@@ -524,19 +524,23 @@
             for d in range(2):
                 piece(d, k, u)
 
-            @pl.when(k < 2)
-            def _():
-                product(owner(u, k + 1))
-
-            @pl.when(k == 2)
-            def _():
-                product(owner(0, 3) if u == 0 else z)
-
-            for step in range(NZ - 1):
-
-                @pl.when(k == step)
+            turn_of = u // 2
+            if u % 2 == 0:
+
+                @pl.when(k < 2)
                 def _():
-                    beside[step, u]()
+                    product(owner(turn_of, k + 1))
+
+                @pl.when(k == 2)
+                def _():
+                    product(owner(0, 3) if turn_of == 0 else z)
+
+            else:
+                for step in range(NZ - 1):
+
+                    @pl.when(k == step)
+                    def _():
+                        beside[step, turn_of]()
 
         return carry
 

time: 151 us -> 152 us (level)
  no operation moved by 1% of the time
where the time goes in v5:
time: 152 us
  Pallas kernels  147 us (97%)
  other arithmetic  2.58 us (2%)
    pallas_call x1, Pallas kernels, on_device(): pl.pallas_call(lambda *refs: kernel(sz, *refs), out_shape=jax.ShapeDtypeS...  147 us

profile of v5, /device:TPU:1, one launch (start us, length us, event | category | flops | bytes accessed | tf_op | source)
XLA Modules:
  0.0 151.9 jit_solution(5905035771539917684)
XLA Ops:
  0.6 0.0 copy-start.1
  0.6 0.0 copy-start
  0.7 1.4 reshape.20.refs_1_
  2.1 147.2 %shard_map.94 = bf16[2,448,512]{2,1,0:T(8,128)(2,1)} custom-call(bf16[64,3584]{1,0:T(8,128)(2,1)} %refs_0_.1, f32[1,3584]{1,0:T(1,128)} %reshape.20.refs_1_, s32[128,128]{1,0:T(8,128)} %bitcast.12, s32[128,128]{1,0:T(8,128)} %bitcast.13, bf16[3584,512]{1,0:T(8,128)(2,1)} %refs_4_.1), custom_call_target="tpu_custom_call" | custom-call | tf_op jit(solution)/shard_map/pallas_call | solution.py:608
  149.3 0.0 copy-done.1
  149.3 0.0 copy-done
  149.3 2.6 %clamp_convert_fusion = (bf16[448,512]{1,0:T(8,128)(2,1)}, bf16[448,512]{1,0:T(8,128)(2,1)}, bf16[448,512]{1,0:T(8,128)(2,1)}) fusion(bf16[448,512]{1,0:T(8,128)(2,1)S(1)} %copy-done, bf16[448,512]{1,0:T(8,128)(2,1)S(1)} %copy-done.1, bf16[2,448,512]{2,1,0:T(8,128)(2,1)} %shard_map.94), kind=kLoop, calls=%fused_computation.3 | loop fusion | flops 3899392 | bytes 3211264 | tf_op jit(solution)/shard_map/convert_element_type | solution.py:664
Async XLA Ops:
  0.6 148.6 %copy-start.1 = (bf16[448,512]{1,0:T(8,128)(2,1)S(1)}, bf16[448,512]{1,0:T(8,128)(2,1)}, u32[]{:S(2)}) copy-start(bf16[448,512]{1,0:T(8,128)(2,1)} %param.13) | copy-start | bytes 1376260
  0.6 148.6 %copy-start = (bf16[448,512]{1,0:T(8,128)(2,1)S(1)}, bf16[448,512]{1,0:T(8,128)(2,1)}, u32[]{:S(2)}) copy-start(bf16[448,512]{1,0:T(8,128)(2,1)} %param.12) | copy-start | bytes 1376260
